TPU v7x, 512 devices: a whole 4x4x16 slice. The times are simulated.
512 devices in a mesh: lat: 8 (over y_hi, x), lon: 16 (over z), grp: 4 (over y_lo, core).
Axes of the slice: x: 4, y: 4 (y_hi: 2, y_lo: 2; y = y_hi * 2 + y_lo), z: 16, core: 2. Of those that a mesh axis runs over, the one named last changes fastest.
Arguments:
- fields: bfloat16 [2, 96, 768, 192], P(None, 'lat', ('lon', 'grp')), may hold values from -6 to 6
- region: int32 [2, 96, 768], P(None, 'lat', ('lon', 'grp')), may hold values from 0 to 2
- bias_index: int32 [72, 72], replicated, may hold values from 0 to 1583
- fine_bias: bfloat16 [16, 1584, 6], P('lat'), may hold values from -4 to 243
- coarse_bias: bfloat16 [8, 1584, 12], P('lat', None, 'grp'), may hold values from -4 to 243
- fine_qkv: bfloat16 [192, 3, 192], replicated, may hold values from -0.4375 to 0.4375
- fine_proj: bfloat16 [192, 192], replicated, may hold values from -0.4375 to 0.4375
- fine_up: bfloat16 [192, 768], replicated, may hold values from -0.4375 to 0.4375
- fine_down: bfloat16 [768, 192], replicated, may hold values from -0.21875 to 0.21875
- merge_weight: bfloat16 [768, 384], replicated, may hold values from -0.21875 to 0.21875
- coarse_qkv: bfloat16 [384, 3, 384], P(None, None, 'grp'), may hold values from -0.3125 to 0.3125
- coarse_proj: bfloat16 [384, 384], P('grp'), may hold values from -0.3125 to 0.3125
- coarse_up: bfloat16 [384, 1536], P(None, 'grp'), may hold values from -0.3125 to 0.3125
- coarse_down: bfloat16 [1536, 384], P('grp'), may hold values from -0.15625 to 0.15625
- out_cotangent: bfloat16 [2, 48, 384, 384], P(None, 'lat', ('lon', 'grp')), may hold values from -6 to 6
Outputs:
- coarse_out: bfloat16 [2, 48, 384, 384], P(None, 'lat', ('lon', 'grp'))
- grad_fields: float32 [2, 96, 768, 192], P(None, 'lat', ('lon', 'grp'))
- grad_fine_bias: float32 [16, 1584, 6], P('lat')
- grad_coarse_bias: float32 [8, 1584, 12], P('lat', None, 'grp')
All inputs are finite; a program needn't handle non-finite values.
Results may differ from a plain program's by a relative error of at most 0.04.
Values may be sent and summed in bfloat16 or wider, within the bound.
A program may use at most 64 MiB of HBM per device.

v0:
```python
import math

import jax
import jax.numpy as jnp
from jax import lax
from jax.sharding import PartitionSpec as P

WZ = 2
WLAT = 6
WLON = 6


EPSILON = 1e-05
NEGATIVE = -1e30
HALF_ROOT = 1.0 / math.sqrt(2.0)
DENSITY = 1.0 / math.sqrt(2.0 * math.pi)


def passed_along(block, axis, distance):
    devices = range(lax.axis_size(axis))
    route = [((i - distance) % len(devices), i) for i in devices]
    return lax.ppermute(block, axis, route)


def layer_norm(values):
    values = values.astype(jnp.float32)
    centred = values - jnp.mean(values, axis=-1, keepdims=True)
    inverse = lax.rsqrt(jnp.mean(centred * centred, axis=-1, keepdims=True) + EPSILON)
    return (centred * inverse, inverse)


def norm_back(normed, inverse, upstream):
    mean_up = jnp.mean(upstream, axis=-1, keepdims=True)
    mean_cross = jnp.mean(upstream * normed, axis=-1, keepdims=True)
    return inverse * (upstream - mean_up - normed * mean_cross)


def gelu_slope(pre_act):
    return (
        0.5 * (1.0 + lax.erf(pre_act * HALF_ROOT))
        + pre_act * jnp.exp(-0.5 * pre_act * pre_act) * DENSITY
    )


def matmul(operand, matrix):
    flat_rows = operand.reshape(-1, operand.shape[-1])
    result = jnp.dot(flat_rows, matrix, preferred_element_type=jnp.float32)
    return result.reshape(operand.shape[:-1] + (matrix.shape[-1],))


def contract(pattern, first_operand, second_operand):
    return jnp.einsum(pattern, first_operand, second_operand, preferred_element_type=jnp.float32)


def unchanged(anything):
    return anything


def to_windows(spatial):
    level_count, row_count, col_count, feature_count = spatial.shape
    blocked = spatial.reshape(
        level_count, row_count // WLAT, WLAT, col_count // WLON, WLON, feature_count
    )
    blocked = jnp.transpose(blocked, (1, 3, 0, 2, 4, 5))
    return blocked.reshape(
        row_count // WLAT, col_count // WLON, level_count * WLAT * WLON, feature_count
    )


def from_windows(windowed):
    lat_blocks, lon_blocks, tokens, feature_count = windowed.shape
    level_count = tokens // (WLAT * WLON)
    blocked = windowed.reshape(lat_blocks, lon_blocks, level_count, WLAT, WLON, feature_count)
    blocked = jnp.transpose(blocked, (2, 0, 3, 1, 4, 5))
    return blocked.reshape(level_count, lat_blocks * WLAT, lon_blocks * WLON, feature_count)


def merge_cells(spatial):
    level_count, row_count, col_count, feature_count = spatial.shape
    blocked = spatial.reshape(level_count, row_count // 2, 2, col_count // 2, 2, feature_count)
    blocked = jnp.transpose(blocked, (0, 1, 3, 4, 2, 5))
    return blocked.reshape(level_count, row_count // 2, col_count // 2, 4 * feature_count)


def split_cells(joined):
    level_count, row_half, col_half, joined_width = joined.shape
    blocked = joined.reshape(level_count, row_half, col_half, 2, 2, joined_width // 4)
    blocked = jnp.transpose(blocked, (0, 1, 4, 2, 3, 5))
    return blocked.reshape(level_count, 2 * row_half, 2 * col_half, joined_width // 4)


def roll_ahead(spatial):
    half_lat = WLAT // 2
    half_lon = WLON // 2
    spatial = jnp.roll(spatial, -(WZ // 2), axis=0)
    arriving = passed_along(spatial[:, :half_lat], "lat", -1)
    spatial = jnp.concatenate([spatial[:, half_lat:], arriving], axis=1)
    arriving = passed_along(spatial[:, :, :half_lon], ("lon", "grp"), -1)
    return jnp.concatenate([spatial[:, :, half_lon:], arriving], axis=2)


def roll_back(spatial):
    half_lat = WLAT // 2
    half_lon = WLON // 2
    arriving = passed_along(spatial[:, :, -half_lon:], ("lon", "grp"), 1)
    spatial = jnp.concatenate([arriving, spatial[:, :, :-half_lon]], axis=2)
    arriving = passed_along(spatial[:, -half_lat:], "lat", 1)
    spatial = jnp.concatenate([arriving, spatial[:, :-half_lat]], axis=1)
    return jnp.roll(spatial, WZ // 2, axis=0)


def attend_forward(normed, qkv_weight, bias_table, position_index, allowed):
    head_count = bias_table.shape[2]
    head_width = qkv_weight.shape[2]
    head_size = head_width // head_count
    scaling = head_size ** (-0.5)
    packed = matmul(normed, qkv_weight.reshape(qkv_weight.shape[0], 3 * head_width)).astype(
        jnp.bfloat16
    )
    packed = packed.reshape(normed.shape[:3] + (3, head_count, head_size))
    queries = packed[:, :, :, 0]
    keys = packed[:, :, :, 1]
    values = packed[:, :, :, 2]
    bias_terms = jnp.take(bias_table, position_index, axis=1).astype(jnp.float32)
    bias_terms = jnp.transpose(bias_terms, (0, 3, 1, 2))[:, None]
    scores = contract("abihd,abjhd->abhij", queries, keys) * scaling + bias_terms
    scores = jnp.where(allowed, scores, NEGATIVE)
    row_peak = jnp.max(scores, axis=-1, keepdims=True)
    weights = jnp.exp(scores - row_peak)
    probabilities = weights / jnp.sum(weights, axis=-1, keepdims=True)
    rounded = probabilities.astype(jnp.bfloat16)
    attended = contract("abhij,abjhd->abihd", rounded, values).astype(jnp.bfloat16)
    return (
        attended.reshape(normed.shape[:3] + (head_width,)),
        (queries, keys, values, probabilities),
    )


def attend_backward(upstream, saved, qkv_weight, position_index, table_length):
    queries, keys, values, probabilities = saved
    head_count = queries.shape[3]
    head_size = queries.shape[4]
    scaling = head_size ** (-0.5)
    upstream = upstream.reshape(upstream.shape[:3] + (head_count, head_size))
    rounded = probabilities.astype(jnp.bfloat16)
    grad_probs = contract("abihd,abjhd->abhij", upstream, values)
    grad_values = contract("abhij,abihd->abjhd", rounded, upstream).astype(jnp.bfloat16)
    grad_scores = probabilities * (
        grad_probs - jnp.sum(grad_probs * probabilities, axis=-1, keepdims=True)
    )
    summed = jnp.sum(grad_scores, axis=1)
    flattened = jnp.transpose(summed, (2, 3, 0, 1)).reshape(position_index.size, -1)
    table_sums = jax.ops.segment_sum(
        flattened, position_index.reshape(-1), num_segments=table_length
    )
    grad_table = jnp.transpose(
        table_sums.reshape(table_length, summed.shape[0], head_count), (1, 0, 2)
    )
    grad_round = grad_scores.astype(jnp.bfloat16)
    grad_queries = (contract("abhij,abjhd->abihd", grad_round, keys) * scaling).astype(jnp.bfloat16)
    grad_keys = (contract("abhij,abihd->abjhd", grad_round, queries) * scaling).astype(jnp.bfloat16)
    grad_packed = jnp.stack([grad_queries, grad_keys, grad_values], axis=3)
    grad_packed = grad_packed.reshape(upstream.shape[:3] + (3 * head_count * head_size,))
    grad_normed = matmul(grad_packed, qkv_weight.reshape(qkv_weight.shape[0], -1).T)
    return (grad_normed, grad_table)


def fine_attend(shifted, allowed, bias_table, position_index, qkv_weight, proj_weight):
    normed, inverse = layer_norm(shifted)
    attended, saved = attend_forward(
        to_windows(normed.astype(jnp.bfloat16)), qkv_weight, bias_table, position_index, allowed
    )
    branch = matmul(attended, proj_weight).astype(jnp.bfloat16)
    return (from_windows(branch), (normed, inverse, saved))


def fine_attend_back(grad_branch, stored, position_index, qkv_weight, proj_weight, table_length):
    normed, inverse, saved = stored
    upstream = matmul(to_windows(grad_branch), proj_weight.T).astype(jnp.bfloat16)
    grad_normed, grad_table = attend_backward(
        upstream, saved, qkv_weight, position_index, table_length
    )
    grad_shifted = norm_back(normed, inverse, from_windows(grad_normed))
    return (grad_shifted.astype(jnp.bfloat16), grad_table)


def fine_mlp(first, up_weight, down_weight, merge_weight):
    normed, inverse = layer_norm(first)
    hidden_pre = matmul(normed.astype(jnp.bfloat16), up_weight)
    hidden = jax.nn.gelu(hidden_pre, approximate=False).astype(jnp.bfloat16)
    second = (first.astype(jnp.float32) + matmul(hidden, down_weight)).astype(jnp.bfloat16)
    joined_norm, joined_inverse = layer_norm(merge_cells(second))
    merged = matmul(joined_norm.astype(jnp.bfloat16), merge_weight).astype(jnp.bfloat16)
    return (merged, (normed, inverse, hidden_pre, joined_norm, joined_inverse))


def fine_mlp_back(grad_merged, stored, up_weight, down_weight, merge_weight):
    normed, inverse, hidden_pre, joined_norm, joined_inverse = stored
    grad_joined = norm_back(joined_norm, joined_inverse, matmul(grad_merged, merge_weight.T))
    grad_second = split_cells(grad_joined)
    grad_hidden = matmul(grad_second.astype(jnp.bfloat16), down_weight.T)
    grad_pre = (grad_hidden * gelu_slope(hidden_pre)).astype(jnp.bfloat16)
    return grad_second + norm_back(normed, inverse, matmul(grad_pre, up_weight.T))


def coarse_forward(base, weights, bias_table, position_index, spread, collect):
    qkv_weight, proj_weight, up_weight, down_weight = weights
    normed, inverse = layer_norm(base)
    attended, saved = attend_forward(
        spread(normed.astype(jnp.bfloat16)), qkv_weight, bias_table, position_index, True
    )
    first = (base.astype(jnp.float32) + collect(matmul(attended, proj_weight))).astype(jnp.bfloat16)
    normed_two, inverse_two = layer_norm(first)
    hidden_pre = matmul(spread(normed_two.astype(jnp.bfloat16)), up_weight)
    hidden = jax.nn.gelu(hidden_pre, approximate=False).astype(jnp.bfloat16)
    second = (first.astype(jnp.float32) + collect(matmul(hidden, down_weight))).astype(jnp.bfloat16)
    return (second, (normed, inverse, saved, normed_two, inverse_two, hidden_pre))


def coarse_backward(upstream, stored, weights, position_index, table_length, spread, collect):
    qkv_weight, proj_weight, up_weight, down_weight = weights
    normed, inverse, saved, normed_two, inverse_two, hidden_pre = stored
    grad_hidden = matmul(spread(upstream), down_weight.T)
    grad_pre = (grad_hidden * gelu_slope(hidden_pre)).astype(jnp.bfloat16)
    grad_first = upstream.astype(jnp.float32) + norm_back(
        normed_two, inverse_two, collect(matmul(grad_pre, up_weight.T))
    )
    grad_attended = matmul(spread(grad_first.astype(jnp.bfloat16)), proj_weight.T).astype(
        jnp.bfloat16
    )
    grad_normed, grad_table = attend_backward(
        grad_attended, saved, qkv_weight, position_index, table_length
    )
    grad_base = grad_first + norm_back(normed, inverse, collect(grad_normed))
    return (grad_base.astype(jnp.bfloat16), grad_table)


def shards(
    fields,
    region,
    bias_index,
    fine_bias,
    coarse_bias,
    fine_qkv,
    fine_proj,
    fine_up,
    fine_down,
    merge_weight,
    coarse_qkv,
    coarse_proj,
    coarse_up,
    coarse_down,
    out_cotangent,
):
    table_length = fine_bias.shape[1]
    shifted = roll_ahead(fields)
    labels = to_windows(region[..., None])[..., 0]
    allowed = (labels[:, :, :, None] == labels[:, :, None, :])[:, :, None]
    fine_branch, fine_stored = fine_attend(
        shifted, allowed, fine_bias, bias_index, fine_qkv, fine_proj
    )
    first = (fields.astype(jnp.float32) + roll_back(fine_branch).astype(jnp.float32)).astype(
        jnp.bfloat16
    )
    merged, mlp_stored = fine_mlp(first, fine_up, fine_down, merge_weight)
    merged_windows = to_windows(merged)
    cotangent_windows = to_windows(out_cotangent)
    gathered = (
        lax.all_gather(coarse_qkv, "grp", axis=2, tiled=True),
        lax.all_gather(coarse_proj, "grp", axis=0, tiled=True),
        lax.all_gather(coarse_up, "grp", axis=1, tiled=True),
        lax.all_gather(coarse_down, "grp", axis=0, tiled=True),
        lax.all_gather(coarse_bias, "grp", axis=2, tiled=True),
    )
    coarse_weights = (gathered[0], gathered[1], gathered[2], gathered[3])
    out_windows, coarse_stored = coarse_forward(
        merged_windows, coarse_weights, gathered[4], bias_index, unchanged, unchanged
    )
    grad_windows, coarse_table = coarse_backward(
        cotangent_windows,
        coarse_stored,
        coarse_weights,
        bias_index,
        table_length,
        unchanged,
        unchanged,
    )
    summed_table = lax.psum(coarse_table, ("lon", "grp"))
    head_share = coarse_bias.shape[2]
    grad_coarse_bias = lax.dynamic_slice_in_dim(
        summed_table, lax.axis_index("grp") * head_share, head_share, 2
    )
    coarse_out = from_windows(out_windows)
    grad_merged = from_windows(grad_windows)
    grad_first = fine_mlp_back(grad_merged, mlp_stored, fine_up, fine_down, merge_weight)
    grad_branch = roll_ahead(grad_first.astype(jnp.bfloat16))
    grad_shifted, fine_table = fine_attend_back(
        grad_branch, fine_stored, bias_index, fine_qkv, fine_proj, table_length
    )
    grad_fine_bias = lax.psum(fine_table, ("lon", "grp"))
    grad_fields = grad_first + roll_back(grad_shifted).astype(jnp.float32)
    return (coarse_out, grad_fields, grad_fine_bias, grad_coarse_bias)


def solution(mesh):
    return jax.shard_map(
        shards,
        mesh=mesh,
        in_specs=(
            P(None, "lat", ("lon", "grp"), None),
            P(None, "lat", ("lon", "grp")),
            P(),
            P("lat", None, None),
            P("lat", None, "grp"),
            P(),
            P(),
            P(),
            P(),
            P(),
            P(None, None, "grp"),
            P("grp", None),
            P(None, "grp"),
            P("grp", None),
            P(None, "lat", ("lon", "grp"), None),
        ),
        out_specs=(
            P(None, "lat", ("lon", "grp"), None),
            P(None, "lat", ("lon", "grp"), None),
            P("lat", None, None),
            P("lat", None, "grp"),
        ),
        check_vma=False,
    )
```

profile of v0, /device:TPU:1, one launch (start us, length us, event | category | flops | bytes accessed | tf_op | source)
XLA Modules:
  0.0 676.7 jit_solution(3112602549085171220)
XLA Ops:
  9.3 7.8 %collective-permute-start = (bf16[2,3,12,192]{3,2,1,0:T(8,128)(2,1)S(1)}, bf16[2,3,12,192]{3,2,1,0:T(8,128)(2,1)S(1)}, u32[]{:S(2)}, u32[]{:S(2)}) collective-permute-start(bf16[2,3,12,192]{3,2,1,0:T(8,128)(2,1)S(1)} %pad_maximum_fusion.11), channel_id=1, source_target_pairs={{64,0},{128,64},{192,128},{256,192},{320,256},{384,320},{448,384},... | collective-permute-start | bytes 82952 | tf_op jit(solution)/shard_map/ppermute | solution.py:22
  19.8 14.1 %gather_fusion = bf16[5184,2,6]{2,1,0:T(2,128)(2,1)} fusion(bf16[2,1584,6]{2,0,1:T(2,128)(2,1)S(1)} %copy.293, s32[6144]{0:T(1024)S(1)} %pad_clamp_fusion), kind=kCustom, calls=%fused_computation | custom fusion | bytes 269568 | tf_op jit(solution)/shard_map/jit(_take)/gather | solution.py:124
  33.9 6.4 copy.294
  41.4 2.9 collective-permute-start.1
  44.4 2.4 collective-permute-done.1
  54.7 18.4 %all_gather.15 = bf16[384,3,384]{0,2,1:T(8,128)(2,1)S(1)} all-gather(bf16[384,3,96]{0,2,1:T(8,128)(2,1)S(1)} %copy-done.37), channel_id=1, replica_groups=mesh['lat'=8,'lon'=16,'grp'=4] {'grp'}, dimensions={2}, use_global_device_ids=true | all-gather | bytes 1105920 | tf_op jit(solution)/shard_map/all_gather | solution.py:269
  76.5 7.5 %all_gather.17 = bf16[384,384]{1,0:T(8,128)(2,1)} all-gather(bf16[96,384]{1,0:T(8,128)(2,1)S(1)} %copy-done.51), channel_id=1, replica_groups=mesh['lat'=8,'lon'=16,'grp'=4] {'grp'}, dimensions={0}, use_global_device_ids=true | all-gather | bytes 368640 | tf_op jit(solution)/shard_map/all_gather | solution.py:270
  84.1 5.3 all_gather.16
  89.7 10.7 %gather_fusion.1 = bf16[5184,12]{1,0:T(8,128)(2,1)S(1)} fusion(bf16[1584,12]{1,0:T(8,128)(2,1)S(1)} %bitcast.232, s32[6144]{0:T(1024)S(1)} %pad_clamp_fusion), kind=kCustom, calls=%fused_computation.1 | custom fusion | bytes 269568 | tf_op jit(solution)/shard_map/jit(_take)/gather | solution.py:124
  105.2 2.7 fusion.31
  114.0 2.5 fusion.169
  116.6 3.8 fusion.261
  128.9 2.1 fusion.258
  132.3 6.7 collective-permute-start.4
  140.1 2.9 collective-permute-start.5
  143.1 2.4 collective-permute-done.5
  158.8 4.4 collective-permute-done.6
  163.3 2.1 collective-permute-start.7
  165.3 2.4 fusion.46
  168.4 2.4 copy.378
  170.8 31.8 %scatter_custom_fusion.1 = f32[1584,12]{1,0:T(8,128)} fusion(s32[5184]{0:T(1024)S(1)} %reshape.676, f32[5184,12]{1,0:T(8,128)} %bitcast.248, f32[]{:T(128)} %constant.46.clone.1), kind=kCustom, calls=%fused_computation.138 | custom fusion | flops 62208 | bytes 76544 | tf_op jit(solution)/shard_map/scatter-add | solution.py:153
  203.0 2.3 copy.343
  205.3 31.3 %scatter_custom_fusion = f32[1584,12]{1,0:T(8,128)S(1)} fusion(s32[5184]{0:T(1024)S(1)} %reshape.676, f32[5184,12]{1,0:T(8,128)} %copy.343, f32[]{:T(128)} %constant.46.clone.1), kind=kCustom, calls=%fused_computation.140 | custom fusion | flops 62208 | bytes 76544 | tf_op jit(solution)/shard_map/scatter-add | solution.py:153
  239.2 427.1 %all-reduce.3.cloned.1.call-done = (f32[2,1584,6]{1,2,0:T(8,128)}, f32[1,1584,12]{2,1,0:T(8,128)}) async-done(((f32[2,1584,6]{1,2,0:T(8,128)}, f32[1,1584,12]{2,1,0:T(8,128)}), (f32[2,1584,6]{1,2,0:T(8,128)}, f32[1,1584,12]{2,1,0:T(8,128)})) %all-reduce.3.cloned.1.call-update) | async-done | bytes 152080 | tf_op jit(solution)/shard_map/psum | solution.py:300
  (328 shorter events, 58.9 us)
Async XLA Ops:
  7.2 102.3 %copy-start = (bf16[768,384]{1,0:T(8,128)(2,1)S(1)}, bf16[768,384]{1,0:T(8,128)(2,1)}, u32[]{:S(2)}) copy-start(bf16[768,384]{1,0:T(8,128)(2,1)} %param.24) | copy-start | bytes 1769476
  7.2 10.1 %copy-start.28 = (s32[72,72]{1,0:T(8,128)S(1)}, s32[72,72]{1,0:T(8,128)}, u32[]{:S(2)}) copy-start(s32[72,72]{1,0:T(8,128)} %param.17) | copy-start | bytes 62212
  7.2 10.2 %copy-start.64 = (s32[2,12,12]{2,0,1:T(2,128)S(1)}, s32[2,12,12]{2,0,1:T(2,128)}, u32[]{:S(2)}) copy-start(s32[2,12,12]{2,0,1:T(2,128)} %param.16) | copy-start | bytes 3460
  7.2 11.2 %copy-start.53 = (bf16[2,1584,6]{1,0,2:T(2,128)(2,1)S(1)}, bf16[2,1584,6]{1,0,2:T(2,128)(2,1)}, u32[]{:S(2)}) copy-start(bf16[2,1584,6]{1,0,2:T(2,128)(2,1)} %param.18) | copy-start | bytes 114052
  7.2 106.8 %all-gather.3.cloned.1.call-start = ((), (), s32[]{:S(2)}) async-start(), calls=%async_computation | async-start | bytes 1474560 | tf_op jit(solution)/shard_map/all_gather | solution.py:271
  7.9 108.6 %all-gather.5.cloned.1.call-start = ((), (), s32[]{:S(2)}) async-start(), calls=%async_computation.1 | async-start | bytes 1474560 | tf_op jit(solution)/shard_map/all_gather | solution.py:272
  9.3 32.1 %collective-permute-start = (bf16[2,3,12,192]{3,2,1,0:T(8,128)(2,1)S(1)}, bf16[2,3,12,192]{3,2,1,0:T(8,128)(2,1)S(1)}, u32[]{:S(2)}, u32[]{:S(2)}) collective-permute-start(bf16[2,3,12,192]{3,2,1,0:T(8,128)(2,1)S(1)} %pad_maximum_fusion.11), channel_id=1, source_target_pairs={{64,0},{128,64},{192,128},{256,192},{320,256},{384,320},{448,384},... | collective-permute-start | bytes 82952 | tf_op jit(solution)/shard_map/ppermute | solution.py:22
  17.2 649.1 %all-reduce.3.cloned.1.call-start = ((), (), s32[]{:S(2)}) async-start(), calls=%async_computation.2 | async-start | bytes 1835008 | tf_op jit(solution)/shard_map/psum | solution.py:300
  17.4 22.9 %copy-start.55 = (pred[72,72]{0,1:T(8,128)(4,1)}, pred[72,72]{0,1:T(8,128)(4,1)S(1)}, u32[]{:S(2)}) copy-start(pred[72,72]{0,1:T(8,128)(4,1)S(1)} %copy.292) | copy-start | bytes 15556
  41.4 9.6 %copy-start.4 = (bf16[192,3,192]{0,2,1:T(8,128)(2,1)}, bf16[192,3,192]{0,2,1:T(8,128)(2,1)S(1)}, u32[]{:S(2)}) copy-start(bf16[192,3,192]{0,2,1:T(8,128)(2,1)S(1)} %copy.284) | copy-start | bytes 663556
  41.4 5.4 collective-permute-start.1
  52.4 24.0 %copy-start.51 = (bf16[96,384]{1,0:T(8,128)(2,1)S(1)}, bf16[96,384]{1,0:T(8,128)(2,1)}, u32[]{:S(2)}) copy-start(bf16[96,384]{1,0:T(8,128)(2,1)} %param.26) | copy-start | bytes 221188
  52.6 31.4 %copy-start.59 = (bf16[1,1584,3]{1,2,0:T(4,128)(2,1)S(1)}, bf16[1,1584,3]{1,2,0:T(4,128)(2,1)}, u32[]{:S(2)}) copy-start(bf16[1,1584,3]{1,2,0:T(4,128)(2,1)} %param.19) | copy-start | bytes 28516
  52.6 31.4 %copy-start.52 = (bf16[2,6,6,384]{3,0,2,1:T(2,128)(2,1)S(1)}, bf16[2,6,6,384]{3,0,2,1:T(2,128)(2,1)}, u32[]{:S(2)}) copy-start(bf16[2,6,6,384]{3,0,2,1:T(2,128)(2,1)} %param.29) | copy-start | bytes 165892
  52.6 20.6 %collective-permute-start.2 = (bf16[2,12,3,192]{3,2,1,0:T(4,128)(2,1)S(1)}, bf16[2,12,3,192]{3,2,1,0:T(4,128)(2,1)S(1)}, u32[]{:S(2)}, u32[]{:S(2)}) collective-permute-start(bf16[2,12,3,192]{3,2,1,0:T(4,128)(2,1)S(1)} %copy.387), channel_id=1, source_target_pairs={{63,0},{0,1},{1,2},{2,3},{3,4},{4,5},{5,6},{6,7},{7,8},{8,9},{9,10... | collective-permute-start | bytes 82952 | tf_op jit(solution)/shard_map/ppermute | solution.py:22
  73.9 10.1 %copy-start.38 = (bf16[2,12,3,192]{3,2,1,0:T(4,128)(2,1)}, bf16[2,12,3,192]{3,2,1,0:T(4,128)(2,1)S(1)}, u32[]{:S(2)}) copy-start(bf16[2,12,3,192]{3,2,1,0:T(4,128)(2,1)S(1)} %collective-permute-done.2) | copy-start | bytes 82948
  74.5 27.4 %collective-permute-start.3 = (bf16[2,3,12,192]{3,2,1,0:T(8,128)(2,1)}, bf16[2,3,12,192]{3,2,1,0:T(8,128)(2,1)}, u32[]{:S(2)}, u32[]{:S(2)}) collective-permute-start(bf16[2,3,12,192]{3,2,1,0:T(8,128)(2,1)} %pad_maximum_fusion.9), channel_id=1, source_target_pairs={{448,0},{0,64},{64,128},{128,192},{192,256},{256,320},{320,384},{3... | collective-permute-start | bytes 82952 | tf_op jit(solution)/shard_map/ppermute | solution.py:22
  132.2 13.7 %copy-start.27 = (bf16[192,192]{1,0:T(8,128)(2,1)S(1)}, bf16[192,192]{1,0:T(8,128)(2,1)}, u32[]{:S(2)}) copy-start(bf16[192,192]{1,0:T(8,128)(2,1)} %param.21) | copy-start | bytes 221188
  132.3 7.8 %collective-permute-start.4 = (bf16[2,3,12,192]{3,2,1,0:T(8,128)(2,1)S(1)}, bf16[2,3,12,192]{3,2,1,0:T(8,128)(2,1)S(1)}, u32[]{:S(2)}, u32[]{:S(2)}) collective-permute-start(bf16[2,3,12,192]{3,2,1,0:T(8,128)(2,1)S(1)} %pad_maximum_fusion.8), channel_id=1, source_target_pairs={{64,0},{128,64},{192,128},{256,192},{320,256},{384,320},{448,384},... | collective-permute-start | bytes 82952 | tf_op jit(solution)/shard_map/ppermute | solution.py:22
  140.1 5.4 collective-permute-start.5
  156.0 9.4 %copy-start.9 = (f32[72,1536]{1,0:T(8,128)S(1)}, f32[72,1536]{1,0:T(8,128)}, u32[]{:S(2)}) copy-start(f32[72,1536]{1,0:T(8,128)} %fusion.169) | copy-start | bytes 1327108
  156.8 6.5 collective-permute-start.6
  163.3 74.4 %collective-permute-start.7 = (bf16[2,3,12,192]{3,2,1,0:T(8,128)(2,1)S(1)}, bf16[2,3,12,192]{3,2,1,0:T(8,128)(2,1)S(1)}, u32[]{:S(2)}, u32[]{:S(2)}) collective-permute-start(bf16[2,3,12,192]{3,2,1,0:T(8,128)(2,1)S(1)} %pad_maximum_fusion.6), channel_id=1, source_target_pairs={{448,0},{0,64},{64,128},{128,192},{192,256},{256,320},{320,384},{3... | collective-permute-start | bytes 82952 | tf_op jit(solution)/shard_map/ppermute | solution.py:22
  168.4 34.2 %copy-start.10 = (f32[2,6,72,72]{2,3,1,0:T(8,128)S(1)}, f32[2,6,72,72]{2,3,1,0:T(8,128)}, u32[]{:S(2)}) copy-start(f32[2,6,72,72]{2,3,1,0:T(8,128)} %get-tuple-element.40) | copy-start | bytes 746500
  (67 other events, 125.9 us)
Sparse Core Ops, SparseCore 0:
  10.2 34.9 all-gather.2
  47.3 32.1 all-gather.4
  237.8 428.4 all-reduce.2
where the time goes:
time: 678 us; the launch traced here: 677 us
  waiting for transfers between devices  438 us (65%)
  other arithmetic  74.5 us (11%)
  local copies, waits for them, and re-layouts  63.4 us (9%)
  blocking collectives  31.2 us (5%)
  starting transfers between devices  28.4 us (4%)
  matrix products  25.6 us (4%)
  between operations  15.5 us (2%)
    psum x1, waiting for transfers between devices, shards(): grad_fine_bias = lax.psum(fine_table, ('lon', 'grp'))  427 us
    scatter-add x2, other arithmetic, attend_backward(): jax.ops.segment_sum(flattened, position_index.reshape(-1), num_segments=t...  63.1 us
    gather x4, local copies, waits for them, and re-layouts, attend_forward(): jnp.take(bias_table, position_index, axis=1).astype(jnp.float32)  32.7 us
    ppermute x8, starting transfers between devices, passed_along(): return lax.ppermute(block, axis, route)  28.3 us
    dot_general x16, matrix products, matmul(): result = jnp.dot(flat_rows, matrix, preferred_element_type=jnp.float32)  19.8 us
    all_gather x1, blocking collectives, shards(): lax.all_gather(coarse_qkv, 'grp', axis=2, tiled=True)  18.4 us
  transfers between devices with their start and end apart: 11, of which 5 were waited for; matrix products, arithmetic and copies ran while one was open for 19% of the time, Pallas kernels for 0%

commit v1 on v0

v1 whole, which is shorter than its diff:
```python
import functools
import math

import jax
import jax.numpy as jnp
import numpy as np
from jax import lax
from jax.experimental import pallas as pl
from jax.experimental.pallas import tpu as pltpu
from jax.sharding import PartitionSpec as P

MESH = pl.DeviceIdType.MESH
F32 = jnp.float32
BF16 = jnp.bfloat16
EPSILON = 1e-05
NEGATIVE = -1e30
HALF_ROOT = 1.0 / math.sqrt(2.0)
DENSITY = 1.0 / math.sqrt(2.0 * math.pi)
SCALING = 32 ** (-0.5)
WIN = 6
HALF = 3
TOK = 72
SIDE = 12
FINE = 4 * TOK
LANES = 128
HIGH = 13
BLOCKS = 16
KEYS = 80
ROWS = 16
UNROLL = 6
LOOP = 1
LATE = 10
HALO = ((0, 64), (64, 64), (128, 32))
HALO_ROWS = 160


def merge_row(level, row, col):
    group = (row % 2) + 2 * (col % 2)
    return group * TOK + level * 36 + (row // 2) * 6 + col // 2


def window_row(level, row, col):
    window = (row // WIN) * 2 + col // WIN
    return window * TOK + level * 36 + (row % WIN) * 6 + col % WIN


def native_row(level, row, col):
    return (row * SIDE + col) * 2 + level


def permutations():
    cells = [(z, i, j) for z in range(2) for i in range(SIDE) for j in range(SIDE)]
    native_to_merge = np.zeros((FINE, FINE), np.float32)
    merge_send = np.zeros((HALO_ROWS, FINE), np.float32)
    merge_to_window = np.zeros((FINE, FINE + HALO_ROWS), np.float32)
    window_send = np.zeros((HALO_ROWS, FINE), np.float32)
    window_to_merge = np.zeros((FINE, FINE + HALO_ROWS), np.float32)
    label_row = np.zeros((FINE, 2 * SIDE), np.float32)
    label_col = np.zeros((FINE, SIDE), np.float32)
    ahead = [0, 0, 0]
    for z, i, j in cells:
        native_to_merge[merge_row(z, i, j), native_row(z, i, j)] = 1
        target = window_row(z, i, j)
        label_row[target, 2 * i + z] = 1
        label_col[target, j] = 1
        source = merge_row((z + 1) % 2, (i + HALF) % SIDE, (j + HALF) % SIDE)
        over_row, over_col = i + HALF >= SIDE, j + HALF >= SIDE
        if not over_row and not over_col:
            merge_to_window[target, source] = 1
            window_to_merge[source, target] = 1
            continue
        kind = 2 if over_row and over_col else (0 if over_row else 1)
        slot = HALO[kind][0] + ahead[kind]
        ahead[kind] += 1
        merge_send[slot, source] = 1
        merge_to_window[target, FINE + slot] = 1
        window_send[slot, target] = 1
        window_to_merge[source, FINE + slot] = 1
    coarse_native = np.zeros((TOK, TOK), np.float32)
    for z in range(2):
        for i in range(6):
            for j in range(6):
                coarse_native[z * 36 + i * 6 + j, (i * 6 + j) * 2 + z] = 1
    return (
        native_to_merge, native_to_merge.T, merge_send, merge_to_window,
        window_send, window_to_merge, coarse_native, coarse_native.T, label_row, label_col,
    )


def dot(a, b):
    return lax.dot_general(a, b, (((1,), (0,)), ((), ())), preferred_element_type=F32)


def dot_nt(a, b):
    return lax.dot_general(a, b, (((1,), (1,)), ((), ())), preferred_element_type=F32)


def dot_tn(a, b):
    return lax.dot_general(a, b, (((0,), (0,)), ((), ())), preferred_element_type=F32)


def rounded(values):
    return values.astype(BF16).astype(F32)


def layer_norm(values):
    centred = values - jnp.mean(values, axis=-1, keepdims=True)
    inverse = lax.rsqrt(jnp.mean(centred * centred, axis=-1, keepdims=True) + EPSILON)
    return centred * inverse, inverse


def norm_back(normed, inverse, upstream):
    mean_up = jnp.mean(upstream, axis=-1, keepdims=True)
    mean_cross = jnp.mean(upstream * normed, axis=-1, keepdims=True)
    return inverse * (upstream - mean_up - normed * mean_cross)


def gelu_both(pre_act):
    half = 0.5 * (1.0 + lax.erf(pre_act * HALF_ROOT))
    slope = half + pre_act * jnp.exp(-0.5 * pre_act * pre_act) * DENSITY
    return pre_act * half, slope


def head_masks(width):
    lane = lax.broadcasted_iota(jnp.int32, (1, width), 1)
    return [(lane >= 32 * h) & (lane < 32 * h + 32) for h in range(width // 32)]


def stack_heads(values, masks):
    return jnp.concatenate([jnp.where(m, values, 0.0) for m in masks], axis=0).astype(BF16)


def unstack_heads(values, masks):
    total = jnp.where(masks[0], values[:TOK], 0.0)
    for h in range(1, len(masks)):
        total = jnp.where(masks[h], values[h * TOK : (h + 1) * TOK], total)
    return total


def softmax(scores):
    weights = jnp.exp(scores - jnp.max(scores, axis=-1, keepdims=True))
    return weights * (1.0 / jnp.sum(weights, axis=-1, keepdims=True))


def table_scatter(grads, chosen, high):
    def step(p, total):
        parts = []
        for half in range(2):
            i = 2 * p + half
            rows = grads[pl.ds(i, ROWS, stride=TOK), :].astype(BF16)
            picked = jnp.broadcast_to(high[pl.ds(i, 1), :], (ROWS, LANES)).astype(BF16)
            zero = jnp.zeros_like(rows)
            parts.append(
                jnp.concatenate(
                    [jnp.where(picked == jnp.asarray(h, BF16), rows, zero) for h in range(HIGH)],
                    axis=0,
                )
            )
        return total + dot(jnp.concatenate(parts, axis=1), chosen[p])

    return lax.fori_loop(0, TOK // 2, step, jnp.zeros((HIGH * ROWS, LANES), F32), unroll=UNROLL)


def table_gather(table, out, chosen, high):
    entries = table[...].astype(BF16)

    def step(p, carry):
        spread = dot_nt(entries, chosen[p])
        for half in range(2):
            i = 2 * p + half
            picked = jnp.broadcast_to(high[pl.ds(i, 1), :], (ROWS, LANES))
            span = slice(half * LANES, (half + 1) * LANES)
            found = spread[:ROWS, span]
            for h in range(1, HIGH):
                found = jnp.where(picked == h, spread[h * ROWS : (h + 1) * ROWS, span], found)
            out[pl.ds(i, ROWS, stride=TOK), :] = found
        return carry

    lax.fori_loop(0, TOK // 2, step, 0, unroll=UNROLL)


def kernel(
    lats,
    rings,
    fields, native_to_merge, merge_send, region, bias_index, fine_bias, coarse_bias,
    label_row, label_col,
    own_qkv, own_proj, own_up, own_down, *rest,
):
    late_hbm, rest = rest[:LATE], rest[LATE:]
    outs, rest = rest[:4], rest[4:]
    late, rest = rest[:LATE], rest[LATE:]
    body(
        lats, rings, fields, native_to_merge, merge_send, region, bias_index, fine_bias,
        coarse_bias, label_row, label_col, own_qkv, own_proj, own_up, own_down,
        late_hbm, late, *late, *outs, *rest,
    )


def body(
    lats, rings,
    fields, native_to_merge, merge_send, region, bias_index, fine_bias, coarse_bias,
    label_row, label_col, own_qkv, own_proj, own_up, own_down,
    late_hbm, late,
    merge_to_window, fine_qkv, fine_proj, window_send, window_to_merge, fine_up, fine_down,
    merge_weight, cotangent, coarse_native,
    coarse_result, grad_result, fine_sums, coarse_sums,
    halo_out, halo_in, got_qkv, got_proj, got_up, got_down, got_cbias,
    label_rows, high, chosen, table, bias, grads_fine, grads_coarse,
    queries, keys, values, probs, score_grads, slope, first_ref, cprobs, cslope,
    spread_ref, label_ref, attended, outer_ref, qkv_grads, cqueries, ckeys, cvalues,
    part_fine, ring_fine, group_fine, final_fine,
    part_coarse, ring_coarse, group_coarse, final_coarse,
    late_sems, halo_send, halo_recv, weight_send, weight_recv, cbias_send, cbias_recv,
    fine_sems, coarse_sems,
):
    lat = lax.axis_index("lat")
    ring = lax.axis_index("lon")
    group = lax.axis_index("grp")
    column = ring * 4 + group
    columns = rings * 4

    def place(row_shift, col_shift):
        row = lax.rem(lat + row_shift + lats, lats)
        col = lax.rem(column + col_shift + columns, columns)
        return {"lat": row, "lon": lax.div(col, 4), "grp": lax.rem(col, 4)}

    before = (place(-1, 0), place(0, -1), place(-1, -1))
    after = (place(1, 0), place(0, 1), place(1, 1))
    core_mate = group + 1 - 2 * lax.rem(group, 2)
    chip_mate = lax.rem(group + 2, 4)
    far_mate = lax.rem(core_mate + 2, 4)
    mates = (core_mate, chip_mate, far_mate)

    barrier = pltpu.get_barrier_semaphore()
    for device in before + after:
        pl.semaphore_signal(barrier, 1, device_id=device, device_id_type=MESH)
    for mate in mates:
        pl.semaphore_signal(barrier, 1, device_id={"grp": mate}, device_id_type=MESH)
    far_lat = lax.rem(lat + lats // 2, lats)
    neighbours = ({"grp": chip_mate}, {"lat": far_lat, "grp": chip_mate})
    pl.semaphore_signal(barrier, 1, device_id=neighbours[1], device_id_type=MESH)
    for step in range(1, rings):
        pl.semaphore_signal(
            barrier, 1, device_id={"lon": lax.rem(ring + step, rings)}, device_id_type=MESH
        )

    def remote(source, target, send, recv, device):
        copy = pltpu.make_async_remote_copy(
            source, target, send, recv, device_id=device, device_id_type=MESH
        )
        copy.start()
        return copy

    def send_halo(number, devices, block):
        halo_out[number] = block.astype(BF16)
        copies = []
        for kind, (start, size) in enumerate(HALO):
            rows = pl.ds(start, size)
            copies.append(
                remote(
                    halo_out.at[number, rows], halo_in.at[number, rows],
                    halo_send.at[number, kind], halo_recv.at[number, kind], devices[kind],
                )
            )
        return copies

    def wait(copies):
        for copy in copies:
            copy.wait()

    loads = [
        pltpu.make_async_copy(source, target, late_sems.at[k])
        for k, (source, target) in enumerate(zip(late_hbm, late))
    ]
    owns = [
        pltpu.make_async_copy(own, got.at[0], late_sems.at[LATE + k])
        for k, (own, got) in enumerate(
            ((own_qkv, got_qkv), (own_proj, got_proj), (own_up, got_up), (own_down, got_down))
        )
    ]
    for copy in loads + owns:
        copy.start()

    tokens = dot(native_to_merge[...], fields[...].astype(F32).reshape(FINE, 192).astype(BF16))
    tokens_half = tokens.astype(BF16)
    first_block = dot(merge_send[...], tokens_half)
    pl.semaphore_wait(barrier, 10 + rings - 1)
    pending = send_halo(0, before, first_block)

    shares = ((own_qkv, got_qkv), (own_proj, got_proj), (own_up, got_up), (own_down, got_down))
    to_chip, to_core, passed = [], [], []

    def half_of(ref, half):
        rows = ref.shape[0] // 2
        return ref.at[pl.ds(half * rows, rows)]

    for k, (own, got) in enumerate(shares):
        to_chip.append(
            [
                remote(
                    half_of(own, half), half_of(got.at[2], half),
                    weight_send.at[k, half], weight_recv.at[k, half], neighbours[half],
                )
                for half in range(2)
            ]
        )
    for k, (own, got) in enumerate(shares):
        to_core.append(
            remote(own, got.at[1], weight_send.at[k, 2], weight_recv.at[k, 2], {"grp": core_mate})
        )

    def pass_on(k):
        got = shares[k][1]
        for copy in to_chip[k]:
            copy.wait_recv()
        passed.append(
            remote(
                got.at[2], got.at[3], weight_send.at[k, 3], weight_recv.at[k, 3], {"grp": core_mate}
            )
        )

    index = bias_index[...]
    high[...] = jnp.zeros_like(high)
    high[:, :TOK] = lax.shift_right_logical(index, 7)
    low = (index & (LANES - 1)).astype(F32).astype(BF16)
    key_row = lax.broadcasted_iota(jnp.int32, (LANES, TOK), 0)
    key_col = lax.broadcasted_iota(jnp.int32, (LANES, TOK), 1)
    identity = jnp.where(key_row == key_col, 1.0, 0.0).astype(BF16)
    low_keys = jnp.where(key_row < TOK, dot_nt(identity, low), -1.0)[:KEYS].astype(BF16)
    query = lax.broadcasted_iota(jnp.int32, (TOK, 2 * LANES), 0)
    lane = lax.broadcasted_iota(jnp.int32, (TOK, 2 * LANES), 1)
    target_query = query - lax.shift_right_logical(lane, 7)
    lane = (lax.broadcasted_iota(jnp.int32, (KEYS, 2 * LANES), 1) & (LANES - 1)).astype(F32)
    blank = jnp.zeros((LANES - KEYS, LANES), BF16)

    def choose(p, carry):
        pick = jnp.where(target_query == 2 * p, 1.0, 0.0).astype(BF16)
        found = jnp.where(dot(low_keys, pick) == lane, 1.0, 0.0).astype(BF16)
        for half in range(2):
            at = half * LANES
            chosen[p, at : at + KEYS, :] = found[:, at : at + LANES]
            chosen[p, at + KEYS : at + LANES, :] = blank
        return carry

    lax.fori_loop(0, TOK // 2, choose, 0, unroll=UNROLL)
    table[...] = jnp.zeros_like(table)
    length = fine_bias.shape[2]
    for h in range(HIGH):
        size = min(LANES, length - h * LANES)
        span = slice(h * LANES, h * LANES + size)
        for head in range(6):
            at = h * ROWS + 2 * head
            table[at : at + 2, :size] = fine_bias[head, :, span].astype(F32)
        at = h * ROWS + 12
        table[at : at + 3, :size] = coarse_bias[0, :, span].astype(F32)
    table_gather(table, bias, chosen, high)
    got_cbias[0] = bias[12 * TOK : 12 * TOK + 224, :].astype(BF16)
    cbias_copies = [
        remote(got_cbias.at[0], got_cbias.at[k + 1], cbias_send.at[k], cbias_recv.at[k], {"grp": mate})
        for k, mate in enumerate(mates)
    ]
    grads_fine[...] = jnp.zeros_like(grads_fine)
    grads_coarse[...] = jnp.zeros_like(grads_coarse)

    fine_masks = head_masks(192)
    for i in range(SIDE):
        label_rows[2 * i : 2 * i + 2, :] = region[i].astype(F32)
    spread_labels = dot(label_row[...], label_rows[...].astype(BF16)) * label_col[...].astype(F32)
    col_labels = jnp.sum(spread_labels, axis=-1, keepdims=True)
    ones = jnp.ones((8, SIDE), BF16)
    spread_ref[...] = spread_labels
    label_ref[...] = col_labels
    loads[0].wait()
    loads[1].wait()
    local = dot(merge_to_window[:, :FINE], tokens_half)
    wait(pending)
    shifted = local + dot(merge_to_window[:, FINE:], halo_in[0])
    fine_normed, fine_inverse = layer_norm(shifted)
    fine_half = fine_normed.astype(BF16)
    for k, ref in enumerate((queries, keys, values)):
        ref[...] = rounded(dot(fine_half, fine_qkv[k]))

    def window_span(w):
        return pl.ds(pl.multiple_of(w * TOK, 8), TOK)

    def attend(w, carry):
        span = window_span(w)
        stacked = stack_heads(queries[span, :], fine_masks)
        scores = dot_nt(stacked, keys[span, :].astype(BF16)) * SCALING
        kind = w // 2
        scores = scores + jnp.concatenate(
            [bias[window_span(2 * h + kind), :TOK] for h in range(6)], axis=0
        )
        row_labels = dot_nt(ones, spread_ref[span, :].astype(BF16))[:1]
        allowed = label_ref[span, :] == row_labels
        scores = jnp.where(allowed[None], scores.reshape(6, TOK, TOK), NEGATIVE)
        weights = softmax(scores.reshape(6 * TOK, TOK))
        probs[w] = weights
        attended[span, :] = unstack_heads(
            dot(weights.astype(BF16), values[span, :].astype(BF16)), fine_masks
        )
        return carry

    lax.fori_loop(0, 4, attend, 0, unroll=LOOP)
    for k in range(2, 5):
        loads[k].wait()
    branch = dot(attended[...].astype(BF16), fine_proj[...]).astype(BF16)
    pending = send_halo(1, after, dot(window_send[...], branch))
    local = tokens + dot(window_to_merge[:, :FINE], branch)
    pass_on(0)
    pass_on(1)
    wait(pending)
    first = rounded(local + dot(window_to_merge[:, FINE:], halo_in[1]))
    first_ref[...] = first

    for k in range(5, 8):
        loads[k].wait()
    normed, inverse = layer_norm(first)
    hidden, slopes = gelu_both(dot(normed.astype(BF16), fine_up[...]))
    slope[...] = slopes
    second = rounded(first + dot_nt(hidden.astype(BF16), fine_down[...]))
    cells = [second[g * TOK : (g + 1) * TOK] for g in range(4)]
    width = 4 * second.shape[1]
    mean = sum(jnp.sum(c, axis=-1, keepdims=True) for c in cells) / width
    cells = [c - mean for c in cells]
    variance = sum(jnp.sum(c * c, axis=-1, keepdims=True) for c in cells) / width
    joined_inverse = lax.rsqrt(variance + EPSILON)
    cells = [c * joined_inverse for c in cells]
    merged = jnp.zeros((TOK, merge_weight.shape[1]), F32)
    for g in range(4):
        merged += dot(cells[g].astype(BF16), merge_weight[g * 192 : (g + 1) * 192, :])
    merged = rounded(merged)
    pass_on(2)
    pass_on(3)

    coarse_masks = head_masks(96)
    loads[8].wait()
    loads[9].wait()
    upstream = dot(
        coarse_native[...], cotangent[...].astype(F32).reshape(TOK, 384).astype(BF16)
    )
    base_normed, base_inverse = layer_norm(merged)
    base_half = base_normed.astype(BF16)
    wait(cbias_copies)

    def arrive(k):
        owns[k].wait()
        to_core[k].wait_recv()
        passed[k].wait_recv()

    arrive(0)
    arrive(1)

    def coarse_attend(g, total):
        q, k, v = (
            rounded(dot_nt(base_half, got_qkv[g, n * 96 : (n + 1) * 96, :])) for n in range(3)
        )
        cqueries[g] = q
        ckeys[g] = k
        cvalues[g] = v
        stacked = stack_heads(q, coarse_masks)
        scores = dot_nt(stacked, k.astype(BF16)) * SCALING
        scores = scores + got_cbias[g].astype(F32)[: 3 * TOK, :TOK]
        weights = softmax(scores)
        cprobs[g] = weights
        seen = unstack_heads(dot(weights.astype(BF16), v.astype(BF16)), coarse_masks)
        return total + dot(seen.astype(BF16), got_proj[g])

    coarse_first = rounded(lax.fori_loop(0, 4, coarse_attend, merged, unroll=LOOP))
    up_normed, up_inverse = layer_norm(coarse_first)
    up_half = up_normed.astype(BF16)
    arrive(2)
    arrive(3)

    def coarse_mlp(g, total):
        hidden, slopes = gelu_both(dot(up_half, got_up[g]))
        cslope[g] = slopes
        return total + dot(hidden.astype(BF16), got_down[g])

    total = lax.fori_loop(0, 4, coarse_mlp, coarse_first, unroll=LOOP)
    coarse_result[...] = total.astype(BF16)

    upstream_half = upstream.astype(BF16)
    blank = jnp.zeros((TOK, 384), F32)

    def coarse_mlp_back(g, total):
        grad_pre = dot_nt(upstream_half, got_down[g]) * cslope[g]
        return total + dot_nt(grad_pre.astype(BF16), got_up[g])

    total = lax.fori_loop(0, 4, coarse_mlp_back, blank, unroll=LOOP)
    grad_first = upstream + norm_back(up_normed, up_inverse, total)
    grad_half = grad_first.astype(BF16)

    def coarse_attend_back(g, total):
        stacked = stack_heads(cqueries[g], coarse_masks)
        weights = cprobs[g]
        outer = stack_heads(rounded(dot_nt(grad_half, got_proj[g])), coarse_masks)
        grad_probs = dot_nt(outer, cvalues[g].astype(BF16))
        grad_scores = weights * (
            grad_probs - jnp.sum(grad_probs * weights, axis=-1, keepdims=True)
        )
        low_bit = lax.rem(group + g, 2)
        high_bit = lax.rem(lax.div(group, 2) + lax.div(g, 2), 2)
        at = pl.multiple_of((2 * high_bit + low_bit) * (3 * TOK), 8)
        grads_coarse[pl.ds(at, 3 * TOK), :TOK] = grad_scores
        grad_scores = grad_scores.astype(BF16)
        grad_v = dot_tn(weights.astype(BF16), outer)
        grad_q = unstack_heads(dot(grad_scores, ckeys[g].astype(BF16)), coarse_masks) * SCALING
        grad_k = dot_tn(grad_scores, stacked) * SCALING
        for n, grad in enumerate((grad_q, grad_k, grad_v)):
            total = total + dot(grad.astype(BF16), got_qkv[g, n * 96 : (n + 1) * 96, :])
        return total

    total = lax.fori_loop(0, 4, coarse_attend_back, blank, unroll=LOOP)
    grad_merged = (grad_first + norm_back(base_normed, base_inverse, total)).astype(BF16)

    joined = [dot_nt(grad_merged, merge_weight[g * 192 : (g + 1) * 192, :]) for g in range(4)]
    mean_up = sum(jnp.sum(j, axis=-1, keepdims=True) for j in joined) / width
    mean_cross = (
        sum(jnp.sum(j * c, axis=-1, keepdims=True) for j, c in zip(joined, cells)) / width
    )
    grad_second = jnp.concatenate(
        [joined_inverse * (j - mean_up - c * mean_cross) for j, c in zip(joined, cells)], axis=0
    )
    grad_pre = dot(grad_second.astype(BF16), fine_down[...]) * slope[...]
    grad_normed = dot_nt(grad_pre.astype(BF16), fine_up[...])
    normed, inverse = layer_norm(first_ref[...])
    grad_fine = grad_second + norm_back(normed, inverse, grad_normed)
    first_ref[...] = grad_fine
    grad_half = grad_fine.astype(BF16)
    pending = send_halo(2, before, dot(merge_send[...], grad_half))

    share = BLOCKS * ROWS // rings

    def sum_start(sums, part, got, sems):
        sums = sums.astype(BF16)
        blank = jnp.zeros((BLOCKS * ROWS - HIGH * ROWS, LANES), BF16)
        part[...] = jnp.concatenate([sums, blank], axis=0).reshape(rings, share, LANES)
        copies = []
        for step in range(1, rings):
            peer = lax.rem(ring + step, rings)
            copies.append(
                remote(
                    part.at[peer], got.at[step], sems.at[0, step], sems.at[1, step], {"lon": peer}
                )
            )
        return copies

    def sum_group(copies, part, got, grouped, sems):
        wait(copies)
        total = part[ring].astype(F32)
        for step in range(1, rings):
            total += got[step].astype(F32)
        grouped[group] = total
        return [
            remote(
                grouped.at[group], grouped.at[group], sems.at[2, k], sems.at[3, k], {"grp": mate}
            )
            for k, mate in enumerate(mates)
        ]

    def sum_spread(copies, grouped, final, sems):
        wait(copies)
        total = grouped[0] + grouped[1] + grouped[2] + grouped[3]
        final[ring] = total.astype(BF16)
        copies = []
        for step in range(1, rings):
            peer = lax.rem(ring + step, rings)
            copies.append(
                remote(
                    final.at[ring], final.at[ring], sems.at[4, step], sems.at[5, step], {"lon": peer}
                )
            )
        return copies

    def sum_end(copies, final):
        wait(copies)
        return final[...].reshape(BLOCKS * ROWS, LANES)

    coarse_copies = sum_start(
        table_scatter(grads_coarse, chosen, high), part_coarse, ring_coarse, coarse_sems
    )

    local = dot(merge_to_window[:, :FINE], grad_half)
    wait(pending)
    grad_branch = local + dot(merge_to_window[:, FINE:], halo_in[2])
    outer_all = rounded(dot_nt(grad_branch.astype(BF16), fine_proj[...]))
    outer_ref[...] = outer_all

    def attend_back(w, carry):
        weights = probs[w]
        span = window_span(w)
        outer = stack_heads(outer_ref[span, :], fine_masks)
        grad_probs = dot_nt(outer, values[span, :].astype(BF16))
        score_grads[w] = weights * (
            grad_probs - jnp.sum(grad_probs * weights, axis=-1, keepdims=True)
        )
        return carry

    lax.fori_loop(0, 4, attend_back, 0, unroll=LOOP)
    for kind in range(2):
        both = score_grads[2 * kind] + score_grads[2 * kind + 1]
        for h in range(6):
            at = (2 * h + kind) * TOK
            grads_fine[at : at + TOK, :TOK] = both[h * TOK : (h + 1) * TOK]
    coarse_copies = sum_group(coarse_copies, part_coarse, ring_coarse, group_coarse, coarse_sems)
    fine_copies = sum_start(
        table_scatter(grads_fine, chosen, high), part_fine, ring_fine, fine_sems
    )

    def project_back(w, carry):
        span = window_span(w)
        outer = stack_heads(outer_ref[span, :], fine_masks)
        stacked = stack_heads(queries[span, :], fine_masks)
        grad_scores = score_grads[w].astype(BF16)
        grad_q = unstack_heads(dot(grad_scores, keys[span, :].astype(BF16)), fine_masks)
        qkv_grads[0, span, :] = grad_q * SCALING
        qkv_grads[1, span, :] = dot_tn(grad_scores, stacked) * SCALING
        qkv_grads[2, span, :] = dot_tn(probs[w].astype(BF16), outer)
        return carry

    lax.fori_loop(0, 4, project_back, 0, unroll=LOOP)
    coarse_copies = sum_spread(coarse_copies, group_coarse, final_coarse, coarse_sems)
    grad_normed = jnp.zeros((FINE, 192), F32)
    for n in range(3):
        grad_normed += dot_nt(qkv_grads[n].astype(BF16), fine_qkv[n])
    grad_shifted = norm_back(fine_normed, fine_inverse, grad_normed).astype(BF16)
    pending = send_halo(3, after, dot(window_send[...], grad_shifted))
    fine_copies = sum_group(fine_copies, part_fine, ring_fine, group_fine, fine_sems)
    local = first_ref[...] + dot(window_to_merge[:, :FINE], grad_shifted)
    wait(pending)
    grad = local + dot(window_to_merge[:, FINE:], halo_in[3])
    fine_copies = sum_spread(fine_copies, group_fine, final_fine, fine_sems)
    grad_result[...] = grad

    sums = sum_end(coarse_copies, final_coarse)
    row = lax.broadcasted_iota(jnp.int32, (8, ROWS), 0)
    col = lax.broadcasted_iota(jnp.int32, (8, ROWS), 1)
    chooser = jnp.where(col == row + 3 * group, 1.0, 0.0).astype(BF16)
    for h in range(HIGH):
        coarse_sums[h] = dot(chooser, sums[h * ROWS : (h + 1) * ROWS])
    for k in range(4):
        for copy in to_chip[k]:
            copy.wait_send()
        to_core[k].wait_send()
        passed[k].wait_send()
    fine_sums[...] = sum_end(fine_copies, final_fine)


def finish(
    grad_result, coarse_result, fine_sums, coarse_sums, merge_to_native, coarse_back,
    coarse_out, grad_fields, grad_fine_bias, grad_coarse_bias,
):
    grad = grad_result[...]
    upper = grad.astype(BF16)
    lower = (grad - upper.astype(F32)).astype(BF16)
    native_grad = dot(merge_to_native[...], upper) + dot(merge_to_native[...], lower)
    grad_fields[...] = native_grad.reshape(SIDE, SIDE, 2, 192)
    result = dot(coarse_back[...], coarse_result[...])
    coarse_out[...] = result.reshape(6, 6, 2, 384).astype(BF16)
    length = grad_fine_bias.shape[2]
    sums = fine_sums[...].astype(F32)
    for h in range(HIGH):
        size = min(LANES, length - h * LANES)
        span = slice(h * LANES, h * LANES + size)
        for head in range(6):
            at = h * ROWS + 2 * head
            grad_fine_bias[head, :, span] = sums[at : at + 2, :size]
        for head in range(3):
            grad_coarse_bias[head, :, span] = coarse_sums[h, head : head + 1, :size]


def shards(
    fields, region, bias_index, fine_bias, coarse_bias, fine_qkv, fine_proj, fine_up, fine_down,
    merge_weight, coarse_qkv, coarse_proj, coarse_up, coarse_down, out_cotangent,
):
    lats = lax.axis_size("lat")
    rings = lax.axis_size("lon")
    share = BLOCKS * ROWS // rings
    (
        native_to_merge, merge_to_native, merge_send, merge_to_window, window_send,
        window_to_merge, coarse_native, coarse_back, label_row, label_col,
    ) = (jnp.asarray(c, BF16) for c in permutations())
    early = (
        jnp.transpose(fields, (1, 2, 0, 3)), native_to_merge, merge_send,
        jnp.transpose(region, (1, 0, 2)), bias_index,
        jnp.transpose(fine_bias, (2, 0, 1)), jnp.transpose(coarse_bias, (0, 2, 1)),
        label_row, label_col,
    )
    owns = (
        jnp.transpose(coarse_qkv, (1, 2, 0)).reshape(3 * 96, 384), coarse_proj, coarse_up,
        coarse_down,
    )
    late = (
        merge_to_window, jnp.transpose(fine_qkv, (1, 0, 2)), fine_proj, window_send,
        window_to_merge, fine_up, fine_down.T, merge_weight,
        jnp.transpose(out_cotangent, (1, 2, 0, 3)), coarse_native,
    )
    vmem = pltpu.VMEM
    dma = pltpu.SemaphoreType.DMA
    sum_buffers = [
        vmem((rings, share, LANES), BF16),
        vmem((rings, share, LANES), BF16),
        vmem((4, share, LANES), F32),
        vmem((rings, share, LANES), BF16),
    ]
    scratch = [vmem(a.shape, a.dtype) for a in late]
    scratch += [
        vmem((4, HALO_ROWS, 192), BF16),
        vmem((4, HALO_ROWS, 192), BF16),
        vmem((4, 3 * 96, 384), BF16),
        vmem((4, 96, 384), BF16),
        vmem((4, 384, 384), BF16),
        vmem((4, 384, 384), BF16),
        vmem((4, 224, LANES), BF16),
        vmem((2 * SIDE, SIDE), F32),
        vmem((TOK, LANES), jnp.int32),
        vmem((TOK // 2, 2 * LANES, LANES), BF16),
        vmem((HIGH * ROWS, LANES), F32),
        vmem((ROWS * TOK, LANES), F32),
        vmem((ROWS * TOK, LANES), F32),
        vmem((ROWS * TOK, LANES), F32),
        vmem((FINE, 192), F32),
        vmem((FINE, 192), F32),
        vmem((FINE, 192), F32),
        vmem((4, 6 * TOK, TOK), F32),
        vmem((4, 6 * TOK, TOK), F32),
        vmem((FINE, 768), F32),
        vmem((FINE, 192), F32),
        vmem((4, 3 * TOK, TOK), F32),
        vmem((4, TOK, 384), F32),
        vmem((FINE, SIDE), F32),
        vmem((FINE, 1), F32),
        vmem((FINE, 192), F32),
        vmem((FINE, 192), F32),
        vmem((3, FINE, 192), F32),
        vmem((4, TOK, 96), F32),
        vmem((4, TOK, 96), F32),
        vmem((4, TOK, 96), F32),
    ]
    scratch += sum_buffers + sum_buffers
    scratch += [
        dma((LATE + 4,)), dma((4, 3)), dma((4, 3)), dma((4, 4)), dma((4, 4)), dma((3,)), dma((3,)),
        dma((6, BLOCKS)), dma((6, BLOCKS)),
    ]
    whole = pl.BlockSpec(memory_space=pltpu.VMEM)
    hbm = pl.BlockSpec(memory_space=pl.ANY)
    coarse_result, grad_result, fine_sums, coarse_sums = pl.pallas_call(
        functools.partial(kernel, lats, rings),
        out_shape=(
            jax.ShapeDtypeStruct((TOK, 384), BF16),
            jax.ShapeDtypeStruct((FINE, 192), F32),
            jax.ShapeDtypeStruct((BLOCKS * ROWS, LANES), BF16),
            jax.ShapeDtypeStruct((HIGH, 8, LANES), F32),
        ),
        in_specs=[whole] * len(early) + [hbm] * (len(owns) + len(late)),
        out_specs=(whole,) * 4,
        scratch_shapes=scratch,
        compiler_params=pltpu.CompilerParams(
            collective_id=0, has_side_effects=True, vmem_limit_bytes=56 * 1024 * 1024
        ),
    )(*early, *owns, *late)
    outs = pl.pallas_call(
        finish,
        out_shape=(
            jax.ShapeDtypeStruct((6, 6, 2, 384), BF16),
            jax.ShapeDtypeStruct((SIDE, SIDE, 2, 192), F32),
            jax.ShapeDtypeStruct((6, 2, fine_bias.shape[1]), F32),
            jax.ShapeDtypeStruct((3, 1, fine_bias.shape[1]), F32),
        ),
        in_specs=[whole] * 6,
        out_specs=(whole,) * 4,
        compiler_params=pltpu.CompilerParams(vmem_limit_bytes=32 * 1024 * 1024),
    )(grad_result, coarse_result, fine_sums, coarse_sums, merge_to_native, coarse_back)
    return (
        jnp.transpose(outs[0], (2, 0, 1, 3)),
        jnp.transpose(outs[1], (2, 0, 1, 3)),
        jnp.transpose(outs[2], (1, 2, 0)),
        jnp.transpose(outs[3], (1, 2, 0)),
    )


def solution(mesh):
    return jax.shard_map(
        shards,
        mesh=mesh,
        in_specs=(
            P(None, "lat", ("lon", "grp"), None),
            P(None, "lat", ("lon", "grp")),
            P(),
            P("lat", None, None),
            P("lat", None, "grp"),
            P(),
            P(),
            P(),
            P(),
            P(),
            P(None, None, "grp"),
            P("grp", None),
            P(None, "grp"),
            P("grp", None),
            P(None, "lat", ("lon", "grp"), None),
        ),
        out_specs=(
            P(None, "lat", ("lon", "grp"), None),
            P(None, "lat", ("lon", "grp"), None),
            P("lat", None, None),
            P("lat", None, "grp"),
        ),
        check_vma=False,
    )
```

time: 678 us -> 84.2 us (0.12)
  waiting for transfers between devices: 438 us -> 0 us
  Pallas kernels: 0 us -> 79.8 us
  other arithmetic: 74.5 us -> 0 us
  local copies, waits for them, and re-layouts: 63.4 us -> 3.43 us
  blocking collectives: 31.2 us -> 0 us
  starting transfers between devices: 28.4 us -> 0 us
  matrix products: 25.6 us -> 0 us
  between operations: 15.5 us -> 0.69 us
    psum x1 -> x0, waiting for transfers between devices: 427 us -> none  [shards(): grad_fine_bias = lax.psum(fine_table, ('lon', 'grp'))]
    pallas_call x0 -> x2, Pallas kernels: none -> 79.8 us  [the longest x1 78.7 us: shards(): pl.pallas_call(functools.partial(kernel, lats, rings), out_shape=(jax.Sha...]
    scatter-add x2 -> x0, other arithmetic: 63.1 us -> none  [attend_backward(): jax.ops.segment_sum(flattened, position_index.reshape(-1), num_segments=t...]
    gather x4 -> x0, local copies, waits for them, and re-layouts: 32.7 us -> none  [attend_forward(): jnp.take(bias_table, position_index, axis=1).astype(jnp.float32)]
    all_gather x3 -> x0, blocking collectives: 31.2 us -> none  [the longest x1 18.4 us: shards(): lax.all_gather(coarse_qkv, 'grp', axis=2, tiled=True)]
    ppermute x8 -> x0, starting transfers between devices: 28.3 us -> none  [passed_along(): return lax.ppermute(block, axis, route)]
    dot_general x26 -> x0, matrix products: 23.6 us -> none  [the longest x16 19.8 us: matmul(): result = jnp.dot(flat_rows, matrix, preferred_element_type=jnp.float32)]
    ppermute x8 -> x0, waiting for transfers between devices: 10.4 us -> none  [passed_along(): return lax.ppermute(block, axis, route)]
  transfers between devices with their start and end apart: 11 -> 0, of which waited for: 5 -> 0; matrix products, arithmetic and copies ran while one was open for 19% -> 0% of each run, Pallas kernels for 0% -> 0%
where the time goes in v1:
time: 84.2 us; the launch traced here: 83.9 us
  Pallas kernels  79.8 us (95%)
  local copies, waits for them, and re-layouts  3.43 us (4%)
    pallas_call x1, Pallas kernels, shards(): pl.pallas_call(functools.partial(kernel, lats, rings), out_shape=(jax.Sha...  78.7 us
    unnamed x12, local copies, waits for them, and re-layouts  3.43 us

profile of v1, /device:TPU:1, one launch (start us, length us, event | category | flops | bytes accessed | tf_op | source)
XLA Modules:
  0.0 83.9 jit_solution(8797607066692865729)
XLA Ops:
  0.6 0.0 copy-start.1
  0.6 0.0 copy-start.5
  0.7 78.7 %shard_map.264 = (bf16[72,384]{1,0:T(8,128)(2,1)}, f32[288,192]{1,0:T(8,128)}, bf16[256,128]{1,0:T(8,128)(2,1)}, f32[13,8,128]{2,1,0:T(8,128)}) custom-call(bf16[12,12,2,192]{3,2,1,0:T(2,128)(2,1)} %bitcast.17, bf16[288,288]{1,0:T(8,128)(2,1)} %constant.20.clone.native_to_merge, bf16[160,288]{1,0:T(8,128)(2,1)} %constant.22.clone.merge_send, ...), custom_call_target="tpu_custom_call" | custom-call | tf_op jit(solution)/shard_map/pallas_call | solution.py:748
  79.3 0.0 copy-done.1
  79.3 0.0 copy-done.5
  79.4 0.0 copy-start
  79.4 1.0 %copy-done = f32[288,192]{1,0:T(8,128)S(1)} copy-done((f32[288,192]{1,0:T(8,128)S(1)}, f32[288,192]{1,0:T(8,128)}, u32[]{:S(2)}) %copy-start) | copy-done | bytes 221208
  80.3 0.0 copy-start.2
  80.3 0.8 copy-done.2
  81.2 0.0 copy-start.3
  81.2 0.8 copy-done.3
  82.0 0.0 copy-start.4
  82.0 0.8 copy-done.4
  82.8 1.1 %shard_map.265 = (bf16[6,6,2,384]{3,2,1,0:T(2,128)(2,1)}, f32[12,12,2,192]{3,2,1,0:T(2,128)}, f32[6,2,1584]{2,1,0:T(2,128)}, f32[3,1,1584]{2,1,0:T(1,128)}) custom-call(f32[288,192]{1,0:T(8,128)S(1)} %copy-done, bf16[72,384]{1,0:T(8,128)(2,1)S(1)} %copy-done.3, bf16[256,128]{1,0:T(8,128)(2,1)S(1)} %copy-done.2, f32[13,8,128]{2,1,0:T(8,128)S(1)} %copy-done.4, ...), custom_call_target="tpu_custom_call" | custom-call | tf_op jit(solution)/shard_map/pallas_call | solution.py:763
Async XLA Ops:
  0.6 78.7 %copy-start.1 = (bf16[288,288]{1,0:T(8,128)(2,1)S(1)}, bf16[288,288]{1,0:T(8,128)(2,1)}, u32[]{:S(2)}) copy-start(bf16[288,288]{1,0:T(8,128)(2,1)} %constant.21.clone.merge_to_native) | copy-start | bytes 497668
  0.6 78.7 %copy-start.5 = (bf16[72,72]{1,0:T(8,128)(2,1)S(1)}, bf16[72,72]{1,0:T(8,128)(2,1)}, u32[]{:S(2)}) copy-start(bf16[72,72]{1,0:T(8,128)(2,1)} %constant.27.clone.coarse_back) | copy-start | bytes 31108
  79.4 1.0 %copy-start = (f32[288,192]{1,0:T(8,128)S(1)}, f32[288,192]{1,0:T(8,128)}, u32[]{:S(2)}) copy-start(f32[288,192]{1,0:T(8,128)} %get-tuple-element.12.grad_result) | copy-start | bytes 663556
  80.3 0.8 %copy-start.2 = (bf16[256,128]{1,0:T(8,128)(2,1)S(1)}, bf16[256,128]{1,0:T(8,128)(2,1)}, u32[]{:S(2)}) copy-start(bf16[256,128]{1,0:T(8,128)(2,1)} %get-tuple-element.14.fine_sums) | copy-start | bytes 196612
  81.2 0.8 copy-start.3
  82.0 0.8 copy-start.4

commit v2 on v1

--- a/solution.py
+++ b/solution.py
@@ -27,9 +27,10 @@
 BLOCKS = 16
 KEYS = 80
 ROWS = 16
-UNROLL = 6
-LOOP = 1
-LATE = 10
+UNROLL = 12
+LOOP = 4
+FETCHED = 19
+EARLY = 9
 HALO = ((0, 64), (64, 64), (128, 32))
 HALO_ROWS = 160
 
@@ -116,9 +117,14 @@
 
 
 def gelu_both(pre_act):
-    half = 0.5 * (1.0 + lax.erf(pre_act * HALF_ROOT))
-    slope = half + pre_act * jnp.exp(-0.5 * pre_act * pre_act) * DENSITY
-    return pre_act * half, slope
+    decay = jnp.exp(-0.5 * pre_act * pre_act)
+    t = 1.0 / (1.0 + (0.3275911 * HALF_ROOT) * jnp.abs(pre_act))
+    poly = 0.5 * 1.061405429
+    for factor in (-1.453152027, 1.421413741, -0.284496736, 0.254829592):
+        poly = poly * t + 0.5 * factor
+    tail = poly * t * decay
+    half = jnp.where(pre_act < 0.0, tail, 1.0 - tail)
+    return pre_act * half, half + pre_act * decay * DENSITY
 
 
 def head_masks(width):
@@ -182,25 +188,20 @@
 def kernel(
     lats,
     rings,
+    own_qkv, own_proj, own_up, own_down, *rest,
+):
+    stored, rest = rest[:FETCHED], rest[FETCHED:]
+    outs, rest = rest[:4], rest[4:]
+    held, rest = rest[:FETCHED], rest[FETCHED:]
+    body(
+        lats, rings, own_qkv, own_proj, own_up, own_down, stored, held, *held, *outs, *rest
+    )
+
+
+def body(
+    lats, rings, own_qkv, own_proj, own_up, own_down, stored, held,
     fields, native_to_merge, merge_send, region, bias_index, fine_bias, coarse_bias,
     label_row, label_col,
-    own_qkv, own_proj, own_up, own_down, *rest,
-):
-    late_hbm, rest = rest[:LATE], rest[LATE:]
-    outs, rest = rest[:4], rest[4:]
-    late, rest = rest[:LATE], rest[LATE:]
-    body(
-        lats, rings, fields, native_to_merge, merge_send, region, bias_index, fine_bias,
-        coarse_bias, label_row, label_col, own_qkv, own_proj, own_up, own_down,
-        late_hbm, late, *late, *outs, *rest,
-    )
-
-
-def body(
-    lats, rings,
-    fields, native_to_merge, merge_send, region, bias_index, fine_bias, coarse_bias,
-    label_row, label_col, own_qkv, own_proj, own_up, own_down,
-    late_hbm, late,
     merge_to_window, fine_qkv, fine_proj, window_send, window_to_merge, fine_up, fine_down,
     merge_weight, cotangent, coarse_native,
     coarse_result, grad_result, fine_sums, coarse_sums,
@@ -231,6 +232,19 @@
     far_mate = lax.rem(core_mate + 2, 4)
     mates = (core_mate, chip_mate, far_mate)
 
+    copies = [
+        pltpu.make_async_copy(source, target, late_sems.at[k])
+        for k, (source, target) in enumerate(zip(stored, held))
+    ]
+    early, loads = copies[:EARLY], copies[EARLY:]
+    owns = [
+        pltpu.make_async_copy(own, got.at[0], late_sems.at[FETCHED + k])
+        for k, (own, got) in enumerate(
+            ((own_qkv, got_qkv), (own_proj, got_proj), (own_up, got_up), (own_down, got_down))
+        )
+    ]
+    for copy in copies:
+        copy.start()
     barrier = pltpu.get_barrier_semaphore()
     for device in before + after:
         pl.semaphore_signal(barrier, 1, device_id=device, device_id_type=MESH)
@@ -268,18 +282,10 @@
         for copy in copies:
             copy.wait()
 
-    loads = [
-        pltpu.make_async_copy(source, target, late_sems.at[k])
-        for k, (source, target) in enumerate(zip(late_hbm, late))
-    ]
-    owns = [
-        pltpu.make_async_copy(own, got.at[0], late_sems.at[LATE + k])
-        for k, (own, got) in enumerate(
-            ((own_qkv, got_qkv), (own_proj, got_proj), (own_up, got_up), (own_down, got_down))
-        )
-    ]
-    for copy in loads + owns:
+    for copy in owns:
         copy.start()
+    for copy in early[:3]:
+        copy.wait()
 
     tokens = dot(native_to_merge[...], fields[...].astype(F32).reshape(FINE, 192).astype(BF16))
     tokens_half = tokens.astype(BF16)
@@ -319,6 +325,8 @@
             )
         )
 
+    for copy in early[3:]:
+        copy.wait()
     index = bias_index[...]
     high[...] = jnp.zeros_like(high)
     high[:, :TOK] = lax.shift_right_logical(index, 7)
@@ -704,7 +712,7 @@
         vmem((4, share, LANES), F32),
         vmem((rings, share, LANES), BF16),
     ]
-    scratch = [vmem(a.shape, a.dtype) for a in late]
+    scratch = [vmem(a.shape, a.dtype) for a in early + late]
     scratch += [
         vmem((4, HALO_ROWS, 192), BF16),
         vmem((4, HALO_ROWS, 192), BF16),
@@ -740,7 +748,7 @@
     ]
     scratch += sum_buffers + sum_buffers
     scratch += [
-        dma((LATE + 4,)), dma((4, 3)), dma((4, 3)), dma((4, 4)), dma((4, 4)), dma((3,)), dma((3,)),
+        dma((FETCHED + 4,)), dma((4, 3)), dma((4, 3)), dma((4, 4)), dma((4, 4)), dma((3,)), dma((3,)),
         dma((6, BLOCKS)), dma((6, BLOCKS)),
     ]
     whole = pl.BlockSpec(memory_space=pltpu.VMEM)
@@ -753,13 +761,13 @@
             jax.ShapeDtypeStruct((BLOCKS * ROWS, LANES), BF16),
             jax.ShapeDtypeStruct((HIGH, 8, LANES), F32),
         ),
-        in_specs=[whole] * len(early) + [hbm] * (len(owns) + len(late)),
+        in_specs=[hbm] * (len(owns) + FETCHED),
         out_specs=(whole,) * 4,
         scratch_shapes=scratch,
         compiler_params=pltpu.CompilerParams(
             collective_id=0, has_side_effects=True, vmem_limit_bytes=56 * 1024 * 1024
         ),
-    )(*early, *owns, *late)
+    )(*owns, *early, *late)
     outs = pl.pallas_call(
         finish,
         out_shape=(
@@ -770,7 +778,7 @@
         ),
         in_specs=[whole] * 6,
         out_specs=(whole,) * 4,
-        compiler_params=pltpu.CompilerParams(vmem_limit_bytes=32 * 1024 * 1024),
+        compiler_params=pltpu.CompilerParams(vmem_limit_bytes=60 * 1024 * 1024),
     )(grad_result, coarse_result, fine_sums, coarse_sums, merge_to_native, coarse_back)
     return (
         jnp.transpose(outs[0], (2, 0, 1, 3)),

time: 84.2 us -> 78.7 us (0.935)
  local copies, waits for them, and re-layouts: 3.43 us -> 0 us
  Pallas kernels: 79.8 us -> 77.6 us
    unnamed x12 -> x0, local copies, waits for them, and re-layouts: 3.43 us -> none
    pallas_call x1, Pallas kernels: 78.7 us -> 75.3 us  [shards(): pl.pallas_call(functools.partial(kernel, lats, rings), out_shape=(jax.Sha...]
    pallas_call x1, Pallas kernels: 1.12 us -> 2.25 us  [shards(): pl.pallas_call(finish, out_shape=(jax.ShapeDtypeStruct((6, 6, 2, 384), BF...]
where the time goes in v2:
time: 78.7 us; the launch traced here: 78.2 us
  Pallas kernels  77.6 us (99%)
    pallas_call x1, Pallas kernels, shards(): pl.pallas_call(functools.partial(kernel, lats, rings), out_shape=(jax.Sha...  75.3 us
    pallas_call x1, Pallas kernels, shards(): pl.pallas_call(finish, out_shape=(jax.ShapeDtypeStruct((6, 6, 2, 384), BF...  2.25 us

profile of v2, /device:TPU:1, one launch (start us, length us, event | category | flops | bytes accessed | tf_op | source)
XLA Modules:
  0.0 78.2 jit_solution(18413716089766430065)
XLA Ops:
  0.6 75.3 %shard_map.264 = (bf16[72,384]{1,0:T(8,128)(2,1)}, f32[288,192]{1,0:T(8,128)}, bf16[256,128]{1,0:T(8,128)(2,1)}, f32[13,8,128]{2,1,0:T(8,128)}) custom-call(bf16[288,384]{1,0:T(8,128)(2,1)} %bitcast.16, bf16[96,384]{1,0:T(8,128)(2,1)} %own_proj.1, bf16[384,384]{1,0:T(8,128)(2,1)} %own_up.1, bf16[384,384]{1,0:T(8,128)(2,1)} %own_down.1, ...), custom_call_target="tpu_custom_call" | custom-call | tf_op jit(solution)/shard_map/pallas_call | solution.py:756
  76.0 2.3 %shard_map.265 = (bf16[6,6,2,384]{3,2,1,0:T(2,128)(2,1)}, f32[12,12,2,192]{3,2,1,0:T(2,128)}, f32[6,2,1584]{2,1,0:T(2,128)}, f32[3,1,1584]{2,1,0:T(1,128)}) custom-call(f32[288,192]{1,0:T(8,128)} %get-tuple-element.12.grad_result, bf16[72,384]{1,0:T(8,128)(2,1)} %get-tuple-element.13.coarse_result, bf16[256,128]{1,0:T(8,128)(2,1)} %get-tuple-element.14.fine_sums, ...), custom_call_target="tpu_custom_call" | custom-call | tf_op jit(solution)/shard_map/pallas_call | solution.py:771

commit v3 on v2

--- a/solution.py
+++ b/solution.py
@@ -29,7 +29,7 @@
 ROWS = 16
 UNROLL = 12
 LOOP = 4
-FETCHED = 19
+FETCHED = 21
 EARLY = 9
 HALO = ((0, 64), (64, 64), (128, 32))
 HALO_ROWS = 160
@@ -203,11 +203,11 @@
     fields, native_to_merge, merge_send, region, bias_index, fine_bias, coarse_bias,
     label_row, label_col,
     merge_to_window, fine_qkv, fine_proj, window_send, window_to_merge, fine_up, fine_down,
-    merge_weight, cotangent, coarse_native,
+    merge_weight, cotangent, coarse_native, coarse_back, merge_to_native,
     coarse_result, grad_result, fine_sums, coarse_sums,
     halo_out, halo_in, got_qkv, got_proj, got_up, got_down, got_cbias,
     label_rows, high, chosen, table, bias, grads_fine, grads_coarse,
-    queries, keys, values, probs, score_grads, slope, first_ref, cprobs, cslope,
+    queries, keys, values, probs, score_grads, slope, first_ref, cprobs, chidden, coarse_ref,
     spread_ref, label_ref, attended, outer_ref, qkv_grads, cqueries, ckeys, cvalues,
     part_fine, ring_fine, group_fine, final_fine,
     part_coarse, ring_coarse, group_coarse, final_coarse,
@@ -442,8 +442,8 @@
     pass_on(3)
 
     coarse_masks = head_masks(96)
-    loads[8].wait()
-    loads[9].wait()
+    for k in range(8, 12):
+        loads[k].wait()
     upstream = dot(
         coarse_native[...], cotangent[...].astype(F32).reshape(TOK, 384).astype(BF16)
     )
@@ -480,22 +480,18 @@
     arrive(2)
     arrive(3)
 
+    upstream_half = upstream.astype(BF16)
+
     def coarse_mlp(g, total):
         hidden, slopes = gelu_both(dot(up_half, got_up[g]))
-        cslope[g] = slopes
-        return total + dot(hidden.astype(BF16), got_down[g])
-
-    total = lax.fori_loop(0, 4, coarse_mlp, coarse_first, unroll=LOOP)
-    coarse_result[...] = total.astype(BF16)
-
-    upstream_half = upstream.astype(BF16)
+        chidden[g] = hidden.astype(BF16)
+        grad_pre = dot_nt(upstream_half, got_down[g]) * slopes
+        return total + dot_nt(grad_pre.astype(BF16), got_up[g])
+
     blank = jnp.zeros((TOK, 384), F32)
-
-    def coarse_mlp_back(g, total):
-        grad_pre = dot_nt(upstream_half, got_down[g]) * cslope[g]
-        return total + dot_nt(grad_pre.astype(BF16), got_up[g])
-
-    total = lax.fori_loop(0, 4, coarse_mlp_back, blank, unroll=LOOP)
+    total = lax.fori_loop(0, 4, coarse_mlp, blank, unroll=LOOP)
+    coarse_ref[...] = coarse_first
+
     grad_first = upstream + norm_back(up_normed, up_inverse, total)
     grad_half = grad_first.astype(BF16)
 
@@ -628,18 +624,25 @@
         return carry
 
     lax.fori_loop(0, 4, project_back, 0, unroll=LOOP)
+    fine_copies = sum_group(fine_copies, part_fine, ring_fine, group_fine, fine_sems)
     coarse_copies = sum_spread(coarse_copies, group_coarse, final_coarse, coarse_sems)
     grad_normed = jnp.zeros((FINE, 192), F32)
     for n in range(3):
         grad_normed += dot_nt(qkv_grads[n].astype(BF16), fine_qkv[n])
     grad_shifted = norm_back(fine_normed, fine_inverse, grad_normed).astype(BF16)
     pending = send_halo(3, after, dot(window_send[...], grad_shifted))
-    fine_copies = sum_group(fine_copies, part_fine, ring_fine, group_fine, fine_sems)
+    fine_copies = sum_spread(fine_copies, group_fine, final_fine, fine_sems)
+
+    total = coarse_ref[...]
+    for g in range(4):
+        total = total + dot(chidden[g], got_down[g])
+    coarse_result[...] = dot(coarse_back[...], total.astype(BF16))
     local = first_ref[...] + dot(window_to_merge[:, :FINE], grad_shifted)
     wait(pending)
     grad = local + dot(window_to_merge[:, FINE:], halo_in[3])
-    fine_copies = sum_spread(fine_copies, group_fine, final_fine, fine_sems)
-    grad_result[...] = grad
+    upper = grad.astype(BF16)
+    lower = (grad - upper.astype(F32)).astype(BF16)
+    grad_result[...] = dot(merge_to_native[...], upper) + dot(merge_to_native[...], lower)
 
     sums = sum_end(coarse_copies, final_coarse)
     row = lax.broadcasted_iota(jnp.int32, (8, ROWS), 0)
@@ -656,16 +659,11 @@
 
 
 def finish(
-    grad_result, coarse_result, fine_sums, coarse_sums, merge_to_native, coarse_back,
+    grad_result, coarse_result, fine_sums, coarse_sums,
     coarse_out, grad_fields, grad_fine_bias, grad_coarse_bias,
 ):
-    grad = grad_result[...]
-    upper = grad.astype(BF16)
-    lower = (grad - upper.astype(F32)).astype(BF16)
-    native_grad = dot(merge_to_native[...], upper) + dot(merge_to_native[...], lower)
-    grad_fields[...] = native_grad.reshape(SIDE, SIDE, 2, 192)
-    result = dot(coarse_back[...], coarse_result[...])
-    coarse_out[...] = result.reshape(6, 6, 2, 384).astype(BF16)
+    grad_fields[...] = grad_result[...].reshape(SIDE, SIDE, 2, 192)
+    coarse_out[...] = coarse_result[...].reshape(6, 6, 2, 384).astype(BF16)
     length = grad_fine_bias.shape[2]
     sums = fine_sums[...].astype(F32)
     for h in range(HIGH):
@@ -702,7 +700,8 @@
     late = (
         merge_to_window, jnp.transpose(fine_qkv, (1, 0, 2)), fine_proj, window_send,
         window_to_merge, fine_up, fine_down.T, merge_weight,
-        jnp.transpose(out_cotangent, (1, 2, 0, 3)), coarse_native,
+        jnp.transpose(out_cotangent, (1, 2, 0, 3)), coarse_native, coarse_back,
+        merge_to_native,
     )
     vmem = pltpu.VMEM
     dma = pltpu.SemaphoreType.DMA
@@ -736,7 +735,8 @@
         vmem((FINE, 768), F32),
         vmem((FINE, 192), F32),
         vmem((4, 3 * TOK, TOK), F32),
-        vmem((4, TOK, 384), F32),
+        vmem((4, TOK, 384), BF16),
+        vmem((TOK, 384), F32),
         vmem((FINE, SIDE), F32),
         vmem((FINE, 1), F32),
         vmem((FINE, 192), F32),
@@ -756,7 +756,7 @@
     coarse_result, grad_result, fine_sums, coarse_sums = pl.pallas_call(
         functools.partial(kernel, lats, rings),
         out_shape=(
-            jax.ShapeDtypeStruct((TOK, 384), BF16),
+            jax.ShapeDtypeStruct((TOK, 384), F32),
             jax.ShapeDtypeStruct((FINE, 192), F32),
             jax.ShapeDtypeStruct((BLOCKS * ROWS, LANES), BF16),
             jax.ShapeDtypeStruct((HIGH, 8, LANES), F32),
@@ -776,10 +776,10 @@
             jax.ShapeDtypeStruct((6, 2, fine_bias.shape[1]), F32),
             jax.ShapeDtypeStruct((3, 1, fine_bias.shape[1]), F32),
         ),
-        in_specs=[whole] * 6,
+        in_specs=[whole] * 4,
         out_specs=(whole,) * 4,
         compiler_params=pltpu.CompilerParams(vmem_limit_bytes=60 * 1024 * 1024),
-    )(grad_result, coarse_result, fine_sums, coarse_sums, merge_to_native, coarse_back)
+    )(grad_result, coarse_result, fine_sums, coarse_sums)
     return (
         jnp.transpose(outs[0], (2, 0, 1, 3)),
         jnp.transpose(outs[1], (2, 0, 1, 3)),

time: 78.7 us -> 77.9 us (0.990)
  no operation moved by 1% of the time
where the time goes in v3:
time: 77.9 us; the launch traced here: 77.8 us
  Pallas kernels  77.1 us (99%)
    pallas_call x1, Pallas kernels, shards(): pl.pallas_call(functools.partial(kernel, lats, rings), out_shape=(jax.Sha...  75.3 us
    pallas_call x1, Pallas kernels, shards(): pl.pallas_call(finish, out_shape=(jax.ShapeDtypeStruct((6, 6, 2, 384), BF...  1.83 us

profile of v3, /device:TPU:1, one launch (start us, length us, event | category | flops | bytes accessed | tf_op | source)
XLA Modules:
  0.0 77.8 jit_solution(497057540006455591)
XLA Ops:
  0.6 75.3 %shard_map.264 = (f32[72,384]{1,0:T(8,128)}, f32[288,192]{1,0:T(8,128)}, bf16[256,128]{1,0:T(8,128)(2,1)}, f32[13,8,128]{2,1,0:T(8,128)}) custom-call(bf16[288,384]{1,0:T(8,128)(2,1)} %bitcast.16, bf16[96,384]{1,0:T(8,128)(2,1)} %own_proj.1, bf16[384,384]{1,0:T(8,128)(2,1)} %own_up.1, bf16[384,384]{1,0:T(8,128)(2,1)} %own_down.1, ...), custom_call_target="tpu_custom_call" | custom-call | tf_op jit(solution)/shard_map/pallas_call | solution.py:756
  75.9 1.8 %shard_map.265 = (bf16[6,6,2,384]{3,2,1,0:T(2,128)(2,1)}, f32[12,12,2,192]{3,2,1,0:T(2,128)}, f32[6,2,1584]{2,1,0:T(2,128)}, f32[3,1,1584]{2,1,0:T(1,128)}) custom-call(f32[288,192]{1,0:T(8,128)} %get-tuple-element.12.grad_result, f32[72,384]{1,0:T(8,128)} %get-tuple-element.13.coarse_result, bf16[256,128]{1,0:T(8,128)(2,1)} %get-tuple-element.14.fine_sums, ...), custom_call_target="tpu_custom_call" | custom-call | tf_op jit(solution)/shard_map/pallas_call | solution.py:771

commit v4 on v3

--- a/solution.py
+++ b/solution.py
@@ -265,18 +265,24 @@
         copy.start()
         return copy
 
+    def together(sent, got, send, recv):
+        return pltpu.make_async_remote_copy(
+            sent, got, send, recv, device_id={"grp": core_mate}, device_id_type=MESH
+        )
+
     def send_halo(number, devices, block):
         halo_out[number] = block.astype(BF16)
-        copies = []
         for kind, (start, size) in enumerate(HALO):
             rows = pl.ds(start, size)
-            copies.append(
-                remote(
-                    halo_out.at[number, rows], halo_in.at[number, rows],
-                    halo_send.at[number, kind], halo_recv.at[number, kind], devices[kind],
-                )
+            remote(
+                halo_out.at[number, rows], halo_in.at[number, rows],
+                halo_send.at[number], halo_recv.at[number], devices[kind],
             )
-        return copies
+        return [
+            together(
+                halo_out.at[number], halo_in.at[number], halo_send.at[number], halo_recv.at[number]
+            )
+        ]
 
     def wait(copies):
         for copy in copies:
@@ -540,42 +546,30 @@
         sums = sums.astype(BF16)
         blank = jnp.zeros((BLOCKS * ROWS - HIGH * ROWS, LANES), BF16)
         part[...] = jnp.concatenate([sums, blank], axis=0).reshape(rings, share, LANES)
-        copies = []
         for step in range(1, rings):
             peer = lax.rem(ring + step, rings)
-            copies.append(
-                remote(
-                    part.at[peer], got.at[step], sems.at[0, step], sems.at[1, step], {"lon": peer}
-                )
-            )
-        return copies
+            remote(part.at[peer], got.at[step], sems.at[0], sems.at[1], {"lon": peer})
+        others = pl.ds(1, rings - 1)
+        return [together(part.at[others], got.at[others], sems.at[0], sems.at[1])]
 
     def sum_group(copies, part, got, grouped, sems):
         wait(copies)
-        total = part[ring].astype(F32)
-        for step in range(1, rings):
-            total += got[step].astype(F32)
+        total = part[ring].astype(F32) + jnp.sum(got[1:].astype(F32), axis=0)
         grouped[group] = total
-        return [
-            remote(
-                grouped.at[group], grouped.at[group], sems.at[2, k], sems.at[3, k], {"grp": mate}
-            )
-            for k, mate in enumerate(mates)
-        ]
+        for mate in mates:
+            remote(grouped.at[group], grouped.at[group], sems.at[2], sems.at[3], {"grp": mate})
+        others = pl.ds(0, 3)
+        return [together(grouped.at[others], grouped.at[others], sems.at[2], sems.at[3])]
 
     def sum_spread(copies, grouped, final, sems):
         wait(copies)
         total = grouped[0] + grouped[1] + grouped[2] + grouped[3]
         final[ring] = total.astype(BF16)
-        copies = []
         for step in range(1, rings):
             peer = lax.rem(ring + step, rings)
-            copies.append(
-                remote(
-                    final.at[ring], final.at[ring], sems.at[4, step], sems.at[5, step], {"lon": peer}
-                )
-            )
-        return copies
+            remote(final.at[ring], final.at[ring], sems.at[4], sems.at[5], {"lon": peer})
+        others = pl.ds(0, rings - 1)
+        return [together(final.at[others], final.at[others], sems.at[4], sems.at[5])]
 
     def sum_end(copies, final):
         wait(copies)
@@ -748,8 +742,8 @@
     ]
     scratch += sum_buffers + sum_buffers
     scratch += [
-        dma((FETCHED + 4,)), dma((4, 3)), dma((4, 3)), dma((4, 4)), dma((4, 4)), dma((3,)), dma((3,)),
-        dma((6, BLOCKS)), dma((6, BLOCKS)),
+        dma((FETCHED + 4,)), dma((4,)), dma((4,)), dma((4, 4)), dma((4, 4)), dma((3,)), dma((3,)),
+        dma((6,)), dma((6,)),
     ]
     whole = pl.BlockSpec(memory_space=pltpu.VMEM)
     hbm = pl.BlockSpec(memory_space=pl.ANY)

time: 77.9 us -> 75.8 us (0.973)
  Pallas kernels: 77.1 us -> 75 us
    pallas_call x1, Pallas kernels: 75.3 us -> 73.2 us  [shards(): pl.pallas_call(functools.partial(kernel, lats, rings), out_shape=(jax.Sha...]
where the time goes in v4:
time: 75.8 us; the launch traced here: 75.7 us
  Pallas kernels  75 us (99%)
    pallas_call x1, Pallas kernels, shards(): pl.pallas_call(functools.partial(kernel, lats, rings), out_shape=(jax.Sha...  73.2 us
    pallas_call x1, Pallas kernels, shards(): pl.pallas_call(finish, out_shape=(jax.ShapeDtypeStruct((6, 6, 2, 384), BF...  1.83 us

profile of v4, /device:TPU:1, one launch (start us, length us, event | category | flops | bytes accessed | tf_op | source)
XLA Modules:
  0.0 75.7 jit_solution(12548310136997718251)
XLA Ops:
  0.6 73.2 %shard_map.264 = (f32[72,384]{1,0:T(8,128)}, f32[288,192]{1,0:T(8,128)}, bf16[256,128]{1,0:T(8,128)(2,1)}, f32[13,8,128]{2,1,0:T(8,128)}) custom-call(bf16[288,384]{1,0:T(8,128)(2,1)} %bitcast.16, bf16[96,384]{1,0:T(8,128)(2,1)} %own_proj.1, bf16[384,384]{1,0:T(8,128)(2,1)} %own_up.1, bf16[384,384]{1,0:T(8,128)(2,1)} %own_down.1, ...), custom_call_target="tpu_custom_call" | custom-call | tf_op jit(solution)/shard_map/pallas_call | solution.py:750
  73.8 1.8 %shard_map.265 = (bf16[6,6,2,384]{3,2,1,0:T(2,128)(2,1)}, f32[12,12,2,192]{3,2,1,0:T(2,128)}, f32[6,2,1584]{2,1,0:T(2,128)}, f32[3,1,1584]{2,1,0:T(1,128)}) custom-call(f32[288,192]{1,0:T(8,128)} %get-tuple-element.12.grad_result, f32[72,384]{1,0:T(8,128)} %get-tuple-element.13.coarse_result, bf16[256,128]{1,0:T(8,128)(2,1)} %get-tuple-element.14.fine_sums, ...), custom_call_target="tpu_custom_call" | custom-call | tf_op jit(solution)/shard_map/pallas_call | solution.py:765

commit v5 on v4

--- a/solution.py
+++ b/solution.py
@@ -27,9 +27,10 @@
 BLOCKS = 16
 KEYS = 80
 ROWS = 16
+SHARE = 64
 UNROLL = 12
 LOOP = 4
-FETCHED = 21
+FETCHED = 23
 EARLY = 9
 HALO = ((0, 64), (64, 64), (128, 32))
 HALO_ROWS = 160
@@ -77,6 +78,13 @@
         merge_to_window[target, FINE + slot] = 1
         window_send[slot, target] = 1
         window_to_merge[source, FINE + slot] = 1
+    by_slot = np.zeros((4 * SHARE, HIGH * ROWS), np.float32)
+    into_fine = np.zeros((HIGH * ROWS, SHARE), np.float32)
+    for h in range(HIGH):
+        for head in range(3):
+            into_fine[h * ROWS + 12 + head, 4 * h + head] = 1
+            for slot in range(4):
+                by_slot[slot * SHARE + 4 * h + head, h * ROWS + 4 * slot + head] = 1
     coarse_native = np.zeros((TOK, TOK), np.float32)
     for z in range(2):
         for i in range(6):
@@ -85,6 +93,7 @@
     return (
         native_to_merge, native_to_merge.T, merge_send, merge_to_window,
         window_send, window_to_merge, coarse_native, coarse_native.T, label_row, label_col,
+        by_slot, into_fine,
     )
 
 
@@ -191,7 +200,7 @@
     own_qkv, own_proj, own_up, own_down, *rest,
 ):
     stored, rest = rest[:FETCHED], rest[FETCHED:]
-    outs, rest = rest[:4], rest[4:]
+    outs, rest = rest[:3], rest[3:]
     held, rest = rest[:FETCHED], rest[FETCHED:]
     body(
         lats, rings, own_qkv, own_proj, own_up, own_down, stored, held, *held, *outs, *rest
@@ -204,13 +213,14 @@
     label_row, label_col,
     merge_to_window, fine_qkv, fine_proj, window_send, window_to_merge, fine_up, fine_down,
     merge_weight, cotangent, coarse_native, coarse_back, merge_to_native,
-    coarse_result, grad_result, fine_sums, coarse_sums,
+    by_slot, into_fine,
+    coarse_result, grad_result, table_sums,
     halo_out, halo_in, got_qkv, got_proj, got_up, got_down, got_cbias,
     label_rows, high, chosen, table, bias, grads_fine, grads_coarse,
     queries, keys, values, probs, score_grads, slope, first_ref, cprobs, chidden, coarse_ref,
     spread_ref, label_ref, attended, outer_ref, qkv_grads, cqueries, ckeys, cvalues,
     part_fine, ring_fine, group_fine, final_fine,
-    part_coarse, ring_coarse, group_coarse, final_coarse,
+    part_coarse, got_coarse,
     late_sems, halo_send, halo_recv, weight_send, weight_recv, cbias_send, cbias_recv,
     fine_sems, coarse_sems,
 ):
@@ -421,6 +431,11 @@
     branch = dot(attended[...].astype(BF16), fine_proj[...]).astype(BF16)
     pending = send_halo(1, after, dot(window_send[...], branch))
     local = tokens + dot(window_to_merge[:, :FINE], branch)
+    for k in range(8, 14):
+        loads[k].wait()
+    upstream = dot(
+        coarse_native[...], cotangent[...].astype(F32).reshape(TOK, 384).astype(BF16)
+    )
     pass_on(0)
     pass_on(1)
     wait(pending)
@@ -448,11 +463,6 @@
     pass_on(3)
 
     coarse_masks = head_masks(96)
-    for k in range(8, 12):
-        loads[k].wait()
-    upstream = dot(
-        coarse_native[...], cotangent[...].astype(F32).reshape(TOK, 384).astype(BF16)
-    )
     base_normed, base_inverse = layer_norm(merged)
     base_half = base_normed.astype(BF16)
     wait(cbias_copies)
@@ -509,10 +519,9 @@
         grad_scores = weights * (
             grad_probs - jnp.sum(grad_probs * weights, axis=-1, keepdims=True)
         )
-        low_bit = lax.rem(group + g, 2)
-        high_bit = lax.rem(lax.div(group, 2) + lax.div(g, 2), 2)
-        at = pl.multiple_of((2 * high_bit + low_bit) * (3 * TOK), 8)
-        grads_coarse[pl.ds(at, 3 * TOK), :TOK] = grad_scores
+        for h in range(3):
+            at = window_span(4 * g + h)
+            grads_coarse[at, :TOK] = grad_scores[h * TOK : (h + 1) * TOK]
         grad_scores = grad_scores.astype(BF16)
         grad_v = dot_tn(weights.astype(BF16), outer)
         grad_q = unstack_heads(dot(grad_scores, ckeys[g].astype(BF16)), coarse_masks) * SCALING
@@ -564,6 +573,8 @@
     def sum_spread(copies, grouped, final, sems):
         wait(copies)
         total = grouped[0] + grouped[1] + grouped[2] + grouped[3]
+        row = lax.broadcasted_iota(jnp.int32, total.shape, 0)
+        total = jnp.where(lax.rem(row, ROWS) < 12, total, grouped[group])
         final[ring] = total.astype(BF16)
         for step in range(1, rings):
             peer = lax.rem(ring + step, rings)
@@ -575,9 +586,19 @@
         wait(copies)
         return final[...].reshape(BLOCKS * ROWS, LANES)
 
-    coarse_copies = sum_start(
-        table_scatter(grads_coarse, chosen, high), part_coarse, ring_coarse, coarse_sems
-    )
+    sums = table_scatter(grads_coarse, chosen, high).astype(BF16)
+    part_coarse[...] = dot(by_slot[...], sums).astype(BF16).reshape(4, SHARE, LANES)
+    for k, mate in enumerate(mates):
+        remote(
+            part_coarse.at[k + 1], got_coarse.at[k + 1], coarse_sems.at[0], coarse_sems.at[1],
+            {"grp": mate},
+        )
+    others = pl.ds(1, 3)
+    coarse_copies = [
+        together(
+            part_coarse.at[others], got_coarse.at[others], coarse_sems.at[0], coarse_sems.at[1]
+        )
+    ]
 
     local = dot(merge_to_window[:, :FINE], grad_half)
     wait(pending)
@@ -601,10 +622,11 @@
         for h in range(6):
             at = (2 * h + kind) * TOK
             grads_fine[at : at + TOK, :TOK] = both[h * TOK : (h + 1) * TOK]
-    coarse_copies = sum_group(coarse_copies, part_coarse, ring_coarse, group_coarse, coarse_sems)
-    fine_copies = sum_start(
-        table_scatter(grads_fine, chosen, high), part_fine, ring_fine, fine_sems
-    )
+    sums = table_scatter(grads_fine, chosen, high)
+    wait(coarse_copies)
+    own_heads = part_coarse[0].astype(F32) + jnp.sum(got_coarse[1:].astype(F32), axis=0)
+    sums = sums + dot(into_fine[...], own_heads.astype(BF16))
+    fine_copies = sum_start(sums, part_fine, ring_fine, fine_sems)
 
     def project_back(w, carry):
         span = window_span(w)
@@ -619,7 +641,6 @@
 
     lax.fori_loop(0, 4, project_back, 0, unroll=LOOP)
     fine_copies = sum_group(fine_copies, part_fine, ring_fine, group_fine, fine_sems)
-    coarse_copies = sum_spread(coarse_copies, group_coarse, final_coarse, coarse_sems)
     grad_normed = jnp.zeros((FINE, 192), F32)
     for n in range(3):
         grad_normed += dot_nt(qkv_grads[n].astype(BF16), fine_qkv[n])
@@ -638,28 +659,22 @@
     lower = (grad - upper.astype(F32)).astype(BF16)
     grad_result[...] = dot(merge_to_native[...], upper) + dot(merge_to_native[...], lower)
 
-    sums = sum_end(coarse_copies, final_coarse)
-    row = lax.broadcasted_iota(jnp.int32, (8, ROWS), 0)
-    col = lax.broadcasted_iota(jnp.int32, (8, ROWS), 1)
-    chooser = jnp.where(col == row + 3 * group, 1.0, 0.0).astype(BF16)
-    for h in range(HIGH):
-        coarse_sums[h] = dot(chooser, sums[h * ROWS : (h + 1) * ROWS])
     for k in range(4):
         for copy in to_chip[k]:
             copy.wait_send()
         to_core[k].wait_send()
         passed[k].wait_send()
-    fine_sums[...] = sum_end(fine_copies, final_fine)
+    table_sums[...] = sum_end(fine_copies, final_fine)
 
 
 def finish(
-    grad_result, coarse_result, fine_sums, coarse_sums,
+    grad_result, coarse_result, table_sums,
     coarse_out, grad_fields, grad_fine_bias, grad_coarse_bias,
 ):
     grad_fields[...] = grad_result[...].reshape(SIDE, SIDE, 2, 192)
     coarse_out[...] = coarse_result[...].reshape(6, 6, 2, 384).astype(BF16)
     length = grad_fine_bias.shape[2]
-    sums = fine_sums[...].astype(F32)
+    sums = table_sums[...].astype(F32)
     for h in range(HIGH):
         size = min(LANES, length - h * LANES)
         span = slice(h * LANES, h * LANES + size)
@@ -667,7 +682,8 @@
             at = h * ROWS + 2 * head
             grad_fine_bias[head, :, span] = sums[at : at + 2, :size]
         for head in range(3):
-            grad_coarse_bias[head, :, span] = coarse_sums[h, head : head + 1, :size]
+            at = h * ROWS + 12 + head
+            grad_coarse_bias[head, :, span] = sums[at : at + 1, :size]
 
 
 def shards(
@@ -679,7 +695,7 @@
     share = BLOCKS * ROWS // rings
     (
         native_to_merge, merge_to_native, merge_send, merge_to_window, window_send,
-        window_to_merge, coarse_native, coarse_back, label_row, label_col,
+        window_to_merge, coarse_native, coarse_back, label_row, label_col, by_slot, into_fine,
     ) = (jnp.asarray(c, BF16) for c in permutations())
     early = (
         jnp.transpose(fields, (1, 2, 0, 3)), native_to_merge, merge_send,
@@ -695,7 +711,7 @@
         merge_to_window, jnp.transpose(fine_qkv, (1, 0, 2)), fine_proj, window_send,
         window_to_merge, fine_up, fine_down.T, merge_weight,
         jnp.transpose(out_cotangent, (1, 2, 0, 3)), coarse_native, coarse_back,
-        merge_to_native,
+        merge_to_native, by_slot, into_fine,
     )
     vmem = pltpu.VMEM
     dma = pltpu.SemaphoreType.DMA
@@ -740,23 +756,22 @@
         vmem((4, TOK, 96), F32),
         vmem((4, TOK, 96), F32),
     ]
-    scratch += sum_buffers + sum_buffers
+    scratch += sum_buffers + [vmem((4, SHARE, LANES), BF16), vmem((4, SHARE, LANES), BF16)]
     scratch += [
         dma((FETCHED + 4,)), dma((4,)), dma((4,)), dma((4, 4)), dma((4, 4)), dma((3,)), dma((3,)),
-        dma((6,)), dma((6,)),
+        dma((6,)), dma((2,)),
     ]
     whole = pl.BlockSpec(memory_space=pltpu.VMEM)
     hbm = pl.BlockSpec(memory_space=pl.ANY)
-    coarse_result, grad_result, fine_sums, coarse_sums = pl.pallas_call(
+    coarse_result, grad_result, table_sums = pl.pallas_call(
         functools.partial(kernel, lats, rings),
         out_shape=(
             jax.ShapeDtypeStruct((TOK, 384), F32),
             jax.ShapeDtypeStruct((FINE, 192), F32),
             jax.ShapeDtypeStruct((BLOCKS * ROWS, LANES), BF16),
-            jax.ShapeDtypeStruct((HIGH, 8, LANES), F32),
         ),
         in_specs=[hbm] * (len(owns) + FETCHED),
-        out_specs=(whole,) * 4,
+        out_specs=(whole,) * 3,
         scratch_shapes=scratch,
         compiler_params=pltpu.CompilerParams(
             collective_id=0, has_side_effects=True, vmem_limit_bytes=56 * 1024 * 1024
@@ -770,10 +785,10 @@
             jax.ShapeDtypeStruct((6, 2, fine_bias.shape[1]), F32),
             jax.ShapeDtypeStruct((3, 1, fine_bias.shape[1]), F32),
         ),
-        in_specs=[whole] * 4,
+        in_specs=[whole] * 3,
         out_specs=(whole,) * 4,
         compiler_params=pltpu.CompilerParams(vmem_limit_bytes=60 * 1024 * 1024),
-    )(grad_result, coarse_result, fine_sums, coarse_sums)
+    )(grad_result, coarse_result, table_sums)
     return (
         jnp.transpose(outs[0], (2, 0, 1, 3)),
         jnp.transpose(outs[1], (2, 0, 1, 3)),

time: 75.8 us -> 70.6 us (0.931)
  the two profiles are of different devices: /device:TPU:1 before, /device:TPU:6 now
where the time goes in v5:
time: 70.6 us; the launch traced here: 70.5 us
  Pallas kernels  69.8 us (99%)
    pallas_call x1, Pallas kernels, shards(): pl.pallas_call(functools.partial(kernel, lats, rings), out_shape=(jax.Sha...  68 us
    pallas_call x1, Pallas kernels, shards(): pl.pallas_call(finish, out_shape=(jax.ShapeDtypeStruct((6, 6, 2, 384), BF...  1.82 us

profile of v5, /device:TPU:6, one launch (start us, length us, event | category | flops | bytes accessed | tf_op | source)
XLA Modules:
  0.0 70.5 jit_solution(12754302717978005383)
XLA Ops:
  0.6 68.0 %shard_map.282 = (f32[72,384]{1,0:T(8,128)}, f32[288,192]{1,0:T(8,128)}, bf16[256,128]{1,0:T(8,128)(2,1)}) custom-call(bf16[288,384]{1,0:T(8,128)(2,1)} %bitcast.16, bf16[96,384]{1,0:T(8,128)(2,1)} %own_proj.1, bf16[384,384]{1,0:T(8,128)(2,1)} %own_up.1, bf16[384,384]{1,0:T(8,128)(2,1)} %own_down.1, bf16[12,12,2,192]{3,2,1,0:T(2,128)(2,1)} %bitcast.17, ...), custom_call_target="tpu_custom_call" | custom-call | tf_op jit(solution)/shard_map/pallas_call | solution.py:766
  68.6 1.8 %shard_map.283 = (bf16[6,6,2,384]{3,2,1,0:T(2,128)(2,1)}, f32[12,12,2,192]{3,2,1,0:T(2,128)}, f32[6,2,1584]{2,1,0:T(2,128)}, f32[3,1,1584]{2,1,0:T(1,128)}) custom-call(f32[288,192]{1,0:T(8,128)} %get-tuple-element.11.grad_result, f32[72,384]{1,0:T(8,128)} %get-tuple-element.12.coarse_result, bf16[256,128]{1,0:T(8,128)(2,1)} %get-tuple-element.13.table_sums), custom_call_target="tpu_custom_call" | custom-call | tf_op jit(solution)/shard_map/pallas_call | solution.py:780

commit v6 on v5

--- a/solution.py
+++ b/solution.py
@@ -215,7 +215,7 @@
     merge_weight, cotangent, coarse_native, coarse_back, merge_to_native,
     by_slot, into_fine,
     coarse_result, grad_result, table_sums,
-    halo_out, halo_in, got_qkv, got_proj, got_up, got_down, got_cbias,
+    halo_out, halo_in, got_all, got_cbias,
     label_rows, high, chosen, table, bias, grads_fine, grads_coarse,
     queries, keys, values, probs, score_grads, slope, first_ref, cprobs, chidden, coarse_ref,
     spread_ref, label_ref, attended, outer_ref, qkv_grads, cqueries, ckeys, cvalues,
@@ -224,6 +224,10 @@
     late_sems, halo_send, halo_recv, weight_send, weight_recv, cbias_send, cbias_recv,
     fine_sems, coarse_sems,
 ):
+    got_qkv = got_all.at[:, pl.ds(0, 288)]
+    got_proj = got_all.at[:, pl.ds(288, 96)]
+    got_up = got_all.at[:, pl.ds(384, 384)]
+    got_down = got_all.at[:, pl.ds(768, 384)]
     lat = lax.axis_index("lat")
     ring = lax.axis_index("lon")
     group = lax.axis_index("grp")
@@ -300,7 +304,7 @@
 
     for copy in owns:
         copy.start()
-    for copy in early[:3]:
+    for copy in early[:3] + owns:
         copy.wait()
 
     tokens = dot(native_to_merge[...], fields[...].astype(F32).reshape(FINE, 192).astype(BF16))
@@ -309,35 +313,38 @@
     pl.semaphore_wait(barrier, 10 + rings - 1)
     pending = send_halo(0, before, first_block)
 
-    shares = ((own_qkv, got_qkv), (own_proj, got_proj), (own_up, got_up), (own_down, got_down))
+    shares = tuple(
+        tuple(got_all.at[slot, pl.ds(start, size)] for slot in range(4))
+        for start, size in ((0, 384), (384, 768))
+    )
     to_chip, to_core, passed = [], [], []
 
     def half_of(ref, half):
         rows = ref.shape[0] // 2
         return ref.at[pl.ds(half * rows, rows)]
 
-    for k, (own, got) in enumerate(shares):
+    for k, (own, mate_slot, chip_slot, far_slot) in enumerate(shares):
         to_chip.append(
             [
                 remote(
-                    half_of(own, half), half_of(got.at[2], half),
+                    half_of(own, half), half_of(chip_slot, half),
                     weight_send.at[k, half], weight_recv.at[k, half], neighbours[half],
                 )
                 for half in range(2)
             ]
         )
-    for k, (own, got) in enumerate(shares):
+    for k, (own, mate_slot, chip_slot, far_slot) in enumerate(shares):
         to_core.append(
-            remote(own, got.at[1], weight_send.at[k, 2], weight_recv.at[k, 2], {"grp": core_mate})
+            remote(own, mate_slot, weight_send.at[k, 2], weight_recv.at[k, 2], {"grp": core_mate})
         )
 
     def pass_on(k):
-        got = shares[k][1]
+        chip_slot, far_slot = shares[k][2:]
         for copy in to_chip[k]:
             copy.wait_recv()
         passed.append(
             remote(
-                got.at[2], got.at[3], weight_send.at[k, 3], weight_recv.at[k, 3], {"grp": core_mate}
+                chip_slot, far_slot, weight_send.at[k, 3], weight_recv.at[k, 3], {"grp": core_mate}
             )
         )
 
@@ -437,7 +444,6 @@
         coarse_native[...], cotangent[...].astype(F32).reshape(TOK, 384).astype(BF16)
     )
     pass_on(0)
-    pass_on(1)
     wait(pending)
     first = rounded(local + dot(window_to_merge[:, FINE:], halo_in[1]))
     first_ref[...] = first
@@ -459,8 +465,7 @@
     for g in range(4):
         merged += dot(cells[g].astype(BF16), merge_weight[g * 192 : (g + 1) * 192, :])
     merged = rounded(merged)
-    pass_on(2)
-    pass_on(3)
+    pass_on(1)
 
     coarse_masks = head_masks(96)
     base_normed, base_inverse = layer_norm(merged)
@@ -468,12 +473,10 @@
     wait(cbias_copies)
 
     def arrive(k):
-        owns[k].wait()
         to_core[k].wait_recv()
         passed[k].wait_recv()
 
     arrive(0)
-    arrive(1)
 
     def coarse_attend(g, total):
         q, k, v = (
@@ -493,8 +496,7 @@
     coarse_first = rounded(lax.fori_loop(0, 4, coarse_attend, merged, unroll=LOOP))
     up_normed, up_inverse = layer_norm(coarse_first)
     up_half = up_normed.astype(BF16)
-    arrive(2)
-    arrive(3)
+    arrive(1)
 
     upstream_half = upstream.astype(BF16)
 
@@ -659,7 +661,7 @@
     lower = (grad - upper.astype(F32)).astype(BF16)
     grad_result[...] = dot(merge_to_native[...], upper) + dot(merge_to_native[...], lower)
 
-    for k in range(4):
+    for k in range(2):
         for copy in to_chip[k]:
             copy.wait_send()
         to_core[k].wait_send()
@@ -725,10 +727,7 @@
     scratch += [
         vmem((4, HALO_ROWS, 192), BF16),
         vmem((4, HALO_ROWS, 192), BF16),
-        vmem((4, 3 * 96, 384), BF16),
-        vmem((4, 96, 384), BF16),
-        vmem((4, 384, 384), BF16),
-        vmem((4, 384, 384), BF16),
+        vmem((4, 1152, 384), BF16),
         vmem((4, 224, LANES), BF16),
         vmem((2 * SIDE, SIDE), F32),
         vmem((TOK, LANES), jnp.int32),

time: 70.6 us -> 70.6 us (level)
  no operation moved by 1% of the time
where the time goes in v6:
time: 70.6 us; the launch traced here: 70.4 us
  Pallas kernels  69.8 us (99%)
    pallas_call x1, Pallas kernels, shards(): pl.pallas_call(functools.partial(kernel, lats, rings), out_shape=(jax.Sha...  67.9 us
    pallas_call x1, Pallas kernels, shards(): pl.pallas_call(finish, out_shape=(jax.ShapeDtypeStruct((6, 6, 2, 384), BF...  1.82 us

profile of v6, /device:TPU:6, one launch (start us, length us, event | category | flops | bytes accessed | tf_op | source)
XLA Modules:
  0.0 70.4 jit_solution(10746545640017535800)
XLA Ops:
  0.6 67.9 %shard_map.282 = (f32[72,384]{1,0:T(8,128)}, f32[288,192]{1,0:T(8,128)}, bf16[256,128]{1,0:T(8,128)(2,1)}) custom-call(bf16[288,384]{1,0:T(8,128)(2,1)} %bitcast.16, bf16[96,384]{1,0:T(8,128)(2,1)} %own_proj.1, bf16[384,384]{1,0:T(8,128)(2,1)} %own_up.1, bf16[384,384]{1,0:T(8,128)(2,1)} %own_down.1, bf16[12,12,2,192]{3,2,1,0:T(2,128)(2,1)} %bitcast.17, ...), custom_call_target="tpu_custom_call" | custom-call | tf_op jit(solution)/shard_map/pallas_call | solution.py:765
  68.6 1.8 %shard_map.283 = (bf16[6,6,2,384]{3,2,1,0:T(2,128)(2,1)}, f32[12,12,2,192]{3,2,1,0:T(2,128)}, f32[6,2,1584]{2,1,0:T(2,128)}, f32[3,1,1584]{2,1,0:T(1,128)}) custom-call(f32[288,192]{1,0:T(8,128)} %get-tuple-element.11.grad_result, f32[72,384]{1,0:T(8,128)} %get-tuple-element.12.coarse_result, bf16[256,128]{1,0:T(8,128)(2,1)} %get-tuple-element.13.table_sums), custom_call_target="tpu_custom_call" | custom-call | tf_op jit(solution)/shard_map/pallas_call | solution.py:779
